TPU v7x, 32 devices: a whole 2x2x4 slice. The times are simulated.
32 devices in a mesh: head: 4 (over y, x), seq: 8 (over z, core).
Axes of the slice: x: 2, y: 2, z: 4, core: 2. Of those that a mesh axis runs over, the one named last changes fastest.
Arguments:
- layer_input: bfloat16 [8192, 768], P('seq'), may hold values from -6 to 6
- cotangent: bfloat16 [8192, 768], P('seq'), may hold values from -6 to 6
- norm1_gain: float32 [768], replicated, may hold values from 0.25 to 1.75
- w_query: bfloat16 [768, 768], P(None, 'head'), may hold values from -0.21875 to 0.21875
- w_key: bfloat16 [768, 768], P(None, 'head'), may hold values from -0.21875 to 0.21875
- w_value: bfloat16 [768, 768], P(None, 'head'), may hold values from -0.21875 to 0.21875
- w_attn_out: bfloat16 [768, 768], P('head'), may hold values from -3 to 3
- bias_table: float32 [32, 12], P(None, 'head'), may hold values from -6 to 6
- norm2_gain: float32 [768], replicated, may hold values from 0.25 to 1.75
- w_router: float32 [768, 8], replicated, may hold values from -0.109375 to 0.109375
- w_expert_in: bfloat16 [8, 768, 3072], P('seq', None, 'head'), may hold values from -0.21875 to 0.21875
- w_expert_out: bfloat16 [8, 3072, 768], P('seq', 'head'), may hold values from -6 to 6
- expert_ids: int32 [8192], P('seq'), may hold values from 0 to 7, as said below
- slot_ids: int32 [8192], P('seq'), may hold values from 0 to 20, as said below
- buckets: int32 [2047], replicated, may hold values from 0 to 31
Outputs:
- layer_output: float32 [8192, 768], P('seq')
- input_grad: float32 [8192, 768], P('seq')
- norm1_gain_grad: float32 [768], replicated
- w_query_grad: float32 [768, 768], P(None, 'head')
- w_key_grad: float32 [768, 768], P(None, 'head')
- w_value_grad: float32 [768, 768], P(None, 'head')
- w_attn_out_grad: float32 [768, 768], P('head')
- bias_table_grad: float32 [32, 12], P(None, 'head')
- norm2_gain_grad: float32 [768], replicated
- w_router_grad: float32 [768, 8], replicated
- w_expert_in_grad: float32 [8, 768, 3072], P('seq', None, 'head')
- w_expert_out_grad: float32 [8, 3072, 768], P('seq', 'head')
Inputs may be any that keep to these rules, and one draw needn't show every extreme that they name: `expert_ids`: in the 1024 tokens of each index of seq one expert, the same for every index, is named by 20 + 1 tokens or more. `slot_ids`: the token's rank, counted from 0 in token order, among the tokens of its index of seq that name the same expert; 20 where that rank is 20 or more (the token is dropped).
All inputs are finite; a program needn't handle non-finite values.
Results may differ from a plain program's by a relative error of at most 0.024.
Values may be sent and summed in bfloat16 or wider, within the bound.
No kernel may reach another device: no remote copies, remote signals or barrier semaphores. Data moves between devices by JAX's collectives and lax.ppermute only.
A program may use at most 192 MiB of HBM per device.

v0:
```python
from functools import partial

import jax
import jax.numpy as jnp
import numpy as np
from jax import lax
from jax.experimental import pallas as pl
from jax.experimental.pallas import tpu as pltpu
from jax.sharding import PartitionSpec as P

CAP = 20
SLOT = 24
EPS = 1e-06
BLOCK = 128
ROWS = 16
EXTRA = 16
TALL = 16
VMEM_LIMIT = 26 * 1024 * 1024
VMEM_ALL = 60 * 1024 * 1024
NO_COST = pl.CostEstimate(flops=1, bytes_accessed=1, transcendentals=0)

f32 = jnp.float32
bf16 = jnp.bfloat16
highest = lax.Precision.HIGHEST


def dot(a, b):
    return jnp.dot(a, b, preferred_element_type=f32)


def dot_nt(a, b, precision=None):
    return lax.dot_general(
        a, b, (((1,), (1,)), ((), ())), precision=precision, preferred_element_type=f32
    )


def dot_tn(a, b, precision=None):
    return lax.dot_general(
        a, b, (((0,), (0,)), ((), ())), precision=precision, preferred_element_type=f32
    )


def iota(shape, dim):
    return lax.broadcasted_iota(jnp.int32, shape, dim)


def split_two(v):
    high = v.astype(bf16)
    return high, (v - high.astype(f32)).astype(bf16)


def shape_of(rows, cols, dtype):
    return jax.ShapeDtypeStruct((rows, cols), dtype)


def spec(memory):
    return pl.BlockSpec(memory_space=memory)


def call(kernel, outs, args, scratch=(), name=None, after=(), moved=1, token=False):
    outs, args = tuple(outs), tuple(args)
    held = sum(int(np.prod(a.shape)) * np.dtype(a.dtype).itemsize for a in args + outs)
    if token:
        outs += (shape_of(8, 128, f32),)
    first_out = len(args) + len(after)

    def body(*refs):
        results = refs[first_out : first_out + len(outs)]
        if token:
            results[-1][...] = jnp.zeros((8, 128), f32)
            results = results[:-1]
        kernel(*refs[: len(args)], *results, *refs[first_out + len(outs) :])

    return pl.pallas_call(
        body,
        out_shape=outs,
        in_specs=[spec(pltpu.VMEM)] * len(args) + [spec(pl.ANY)] * len(after),
        out_specs=tuple(spec(pltpu.VMEM) for _ in outs),
        scratch_shapes=list(scratch),
        compiler_params=pltpu.CompilerParams(
            vmem_limit_bytes=VMEM_LIMIT if 2 * held < VMEM_LIMIT else VMEM_ALL
        ),
        cost_estimate=pl.CostEstimate(flops=1, bytes_accessed=moved, transcendentals=0),
        name=name,
    )(*args, *after)


def slot_rows(ids, slots, rows, each):
    cell = jnp.where(slots < CAP, ids * each + slots, -1)
    return (iota((rows, cell.shape[1]), 0) == cell).astype(f32)


def place_kernel(x_ref, cot_ref, ids_ref, slots_ref, *refs, heads):
    w_parts = refs[:heads]
    sel_in, sel_up, place, place_c, x_c, cot_c, w_ref, place_s = refs[heads:]
    head = lax.axis_index("head")
    part = x_c.shape[0]
    slot_hot = slot_rows(ids_ref[...], slots_ref[...], sel_in.shape[0], SLOT)
    place_s[...] = jnp.transpose(slot_hot)
    slot_low = slot_hot.astype(bf16)
    sel_in[...] = dot(slot_low, x_ref[...]).astype(bf16)
    sel_up[...] = dot(slot_low, cot_ref[...]).astype(bf16)
    place[...] = place_s[...].astype(bf16)
    mine = pl.ds(pl.multiple_of(head * part, part), part)
    place_c[...] = place_s[mine, :].astype(bf16)
    x_c[...] = x_ref[mine, :]
    cot_c[...] = cot_ref[mine, :]
    inner = w_parts[0].shape[0]
    for d in range(heads):
        rows = pl.ds(pl.multiple_of((head ^ d) * inner, inner), inner)
        w_ref[rows, :] = w_parts[d][...]


def attend_kernel(*refs):
    given, refs = refs[:9], refs[9:]
    low_ref, prob_ref, att_ref, attt_ref, sel_ref = refs[:5]
    q_s, kt_s, v_s, bias_s, skew_s, slot_s, score_s = refs[5:12]
    here, sems = refs[12:21], refs[21]
    x_ref, gain_ref, wq_ref, wk_ref, wv_ref, table_ref, buckets_ref, ids_ref, slots_ref = here
    copies = [
        pltpu.make_async_copy(far, near, sems.at[i])
        for i, (far, near) in enumerate(zip(given, here))
    ]
    tokens = x_ref.shape[0]
    inner = wq_ref.shape[0]
    count = q_s.shape[0]
    width = inner // count
    span = skew_s.shape[2]
    tall = 2 * BLOCK
    for copy in copies:
        copy.start()
    for copy in copies[5:]:
        copy.wait()
    slot_s[...] = slot_rows(ids_ref[...], slots_ref[...], slot_s.shape[0], CAP).astype(bf16)
    offsets = buckets_ref.shape[1]
    bucket_hot = (iota((table_ref.shape[1], offsets), 0) == buckets_ref[...]).astype(f32)
    bias_s[...] = jnp.zeros_like(bias_s)
    bias_s[:count, :offsets] = jnp.dot(
        table_ref[...], bucket_hot, precision=highest, preferred_element_type=f32
    )
    for copy in copies[:2]:
        copy.wait()
    for i in range(0, tokens, 256):
        rows = pl.ds(i, 256)
        x = x_ref[rows, :].astype(f32)
        inverse = lax.rsqrt(jnp.mean(x * x, axis=-1, keepdims=True) + EPS)
        low_ref[rows, :] = (x * inverse * gain_ref[...]).astype(bf16)
    for copy in copies[2:5]:
        copy.wait()
    low = low_ref[...]
    q = dot_nt(low, wq_ref[...]).astype(bf16) * bf16(width ** (-0.5))
    kt_s[...] = dot_nt(wk_ref[...], low).astype(bf16)
    v = dot_nt(low, wv_ref[...]).astype(bf16)
    for h in range(count):
        cols = slice(h * width, (h + 1) * width)
        q_s[h] = q[:, cols]
        v_s[h] = v[:, cols]

    blocks = tokens // tall
    half = sel_ref.shape[0]

    def lay_bias(h):
        skew_s[h % 2] = pltpu.roll(
            jnp.broadcast_to(bias_s[h : h + 1, :], skew_s.shape[1:]),
            span - (BLOCK - 1), 1, stride=1, stride_axis=0,
        )

    def scores(h, n):
        score_s[n % 2] = dot(
            q_s[h, pl.ds(n * tall, tall), :], kt_s[h * width : (h + 1) * width, :]
        )

    def weights(h, n):
        for j in range(0, tall, ROWS):
            row = n * tall + j
            first = tokens - BLOCK - row // BLOCK * BLOCK
            bias = skew_s[h % 2, j % BLOCK : j % BLOCK + ROWS, first : first + tokens]
            score = score_s[n % 2, j : j + ROWS, :] + bias
            weight = jnp.exp(score - jnp.max(score, axis=-1, keepdims=True))
            total = jnp.sum(weight, axis=-1, keepdims=True)
            prob_ref[h, pl.ds(row, ROWS), :] = (weight * (1.0 / total)).astype(bf16)

    lay_bias(0)
    scores(0, 0)
    for h in range(count):
        for n in range(blocks):
            if n + 1 < blocks:
                scores(h, n + 1)
            elif h + 1 < count:
                lay_bias(h + 1)
                scores(h + 1, 0)
            weights(h, n)
        att = dot(prob_ref[h], v_s[h])
        att_low = att.astype(bf16)
        att_ref[h] = att_low
        attt_ref[h * width : (h + 1) * width, :] = jnp.transpose(att).astype(bf16)
        picked = dot(slot_s[...], att_low).astype(bf16)
        for part in range(2):
            start = part * inner + h * width
            sel_ref[:, start : start + width] = picked[part * half : (part + 1) * half]


def pass_kernel(given, passed):
    passed[...] = given[...]


def widen(rows, wide_s):
    wide_s[...] = jnp.zeros_like(wide_s)
    for e in range(rows.shape[0] // CAP):
        wide_s[e * SLOT : e * SLOT + CAP, :] = rows[e * CAP : (e + 1) * CAP]
    return wide_s[...]


def packed_width(width):
    return 2 * width + width // 2 + 128


def short_rows(width):
    each = width // 2
    for i in range(CAP - TALL):
        for k in range(4):
            yield TALL + i, slice(k * each, (k + 1) * each), 4 * i + k


def route_kernel(*refs, shards, heads):
    att_parts, w_ref = refs[:heads], refs[heads]
    (sel_in, sel_up, gain_ref, router_ref, att_t, hidden_ref, normed_ref, probs_ref, att_on
     ) = refs[heads + 1 : heads + 10]
    pieces = refs[heads + 10 : heads + 10 + shards]
    att_s, pay_s, wide_s, pack_s = refs[heads + 10 + shards :]
    head = lax.axis_index("head")
    half = att_parts[0].shape[0]
    inner = w_ref.shape[0] // heads
    for d in range(heads):
        att_s[d, 0:half, :] = att_parts[d][:, 0:inner]
        att_s[d, half : 2 * half, :] = att_parts[d][:, inner : 2 * inner]
    mixed = None
    for k in range(heads):
        term = dot(att_s[head ^ k], w_ref[k * inner : (k + 1) * inner, :])
        mixed = term if mixed is None else mixed + term
    hidden = sel_in[...].astype(f32) + widen(mixed, wide_s)
    hidden_ref[...] = hidden
    inverse = lax.rsqrt(jnp.mean(hidden * hidden, axis=-1, keepdims=True) + EPS)
    normed = hidden * inverse * gain_ref[...]
    normed_ref[...] = normed
    logits = dot_nt(normed, router_ref[...], highest)
    logits = logits - jnp.max(logits, axis=-1, keepdims=True)
    powers = jnp.exp(logits)
    probs = powers / jnp.sum(powers, axis=-1, keepdims=True)
    probs_ref[...] = probs
    gate = jnp.sum(jnp.where(chosen_of(probs.shape), probs, 0.0), axis=-1, keepdims=True)
    high = gate.astype(bf16).astype(f32)
    lane = iota((gate.shape[0], 128), 1)
    width = normed.shape[1]
    rest = gate - high
    first_gates = jnp.where(lane == 0, high, jnp.where(lane == 1, rest, 0.0))
    last_gates = jnp.where(lane == 2, high, jnp.where(lane == 3, rest, 0.0))
    pay_s[:, :width] = normed
    pay_s[:, width:] = sel_up[...].astype(f32)
    full, side = 2 * width, 2 * width + width // 2
    for e in range(shards):
        rows, packed = e * SLOT, e * TALL
        pack_s[packed : packed + TALL, :full] = pay_s[rows : rows + TALL, :]
        for row, lanes, to in short_rows(width):
            pack_s[packed + to : packed + to + 1, full:side] = pay_s[
                rows + row : rows + row + 1, lanes
            ]
        pack_s[packed : packed + 8, side:] = (
            first_gates[rows : rows + 8] + last_gates[rows + TALL : rows + SLOT]
        )
        pack_s[packed + 8 : packed + TALL, side:] = first_gates[rows + 8 : rows + TALL]
    shard = lax.axis_index("seq")
    for j in range(shards):
        first = pl.multiple_of((shard ^ j) * TALL, TALL)
        pieces[j][...] = pack_s[pl.ds(first, TALL), :].astype(bf16)
    att_on[...] = att_t[...]


def chosen_of(shape):
    expert = iota(shape, 1) * SLOT
    slot_row = iota(shape, 0)
    return (slot_row >= expert) & (slot_row < expert + SLOT)


def far_first(count):
    return sorted(range(count), key=lambda d: (-(d // 2), -d if d < 2 else d))


def by_partner(refs):
    return [ref for _, ref in sorted(zip(far_first(len(refs)), refs), key=lambda t: t[0])]


def expert_kernel(*refs, shards, heads):
    parts = by_partner(refs[:shards])
    w_in, w_out = refs[shards : shards + 2]
    chunks = refs[shards + 2 : shards + 2 + heads]
    x_ref, act_ref, pre_ref, out_ref, pay_s, gate_s, both_s = refs[shards + 2 + heads :]
    head = lax.axis_index("head")
    width = x_ref.shape[1]
    full, side = 2 * width, 2 * width + width // 2
    for j in range(shards):
        rows = j * SLOT
        part = parts[j][...].astype(f32)
        pay_s[rows : rows + TALL, :] = part[:, :full]
        pay_s[rows + TALL : rows + SLOT, :] = jnp.zeros((SLOT - TALL, full), f32)
        for row, lanes, place in short_rows(width):
            pay_s[rows + row : rows + row + 1, lanes] = part[place : place + 1, full:side]
        gate_s[rows : rows + TALL, :] = part[:, side : side + 1] + part[:, side + 1 : side + 2]
        gate_s[rows + TALL : rows + SLOT, :] = (
            part[:8, side + 2 : side + 3] + part[:8, side + 3 : side + 4]
        )
    x = pay_s[:, :width].astype(bf16)
    up = pay_s[:, width:]
    gate = gate_s[...]
    out_low = (gate * up).astype(bf16)
    pre = dot(x, w_in[...])
    cdf = 0.5 * (1.0 + lax.erf(pre * (0.5**0.5)))
    act = (pre * cdf).astype(bf16)
    slope = cdf + pre * jnp.exp(-0.5 * pre * pre) * ((2.0 * np.pi) ** (-0.5))
    pre_low = (dot_nt(out_low, w_out[...]) * slope).astype(bf16)
    both = (dot(act, w_out[...]), dot_nt(pre_low, w_in[...]))
    part = both_s.shape[2]
    for k in range(heads):
        start = k % (heads // 2) * part
        for j in range(shards):
            both_s[k, j * CAP : (j + 1) * CAP, :] = both[k // (heads // 2)][
                j * SLOT : j * SLOT + CAP, start : start + part
            ]
    for d in range(heads):
        chunks[d][...] = both_s[head ^ d].astype(bf16)
    pre_ref[...] = pre_low
    out_ref[...] = out_low
    x_ref[...] = x
    act_ref[...] = act


def expert_grad_kernel(x_ref, pre_ref, act_ref, out_ref, in_grad, out_grad):
    in_grad[0] = dot_tn(x_ref[...], pre_ref[...])
    out_grad[0] = dot_tn(act_ref[...], out_ref[...])


def sum_kernel(att_ref, *refs, heads):
    parts, att_on, pieces, sum_s = refs[:heads], refs[heads], refs[heads + 1 : -1], refs[-1]
    att_on[...] = att_ref[...]
    total = parts[0][...].astype(f32)
    for d in range(1, heads):
        total = total + parts[d][...].astype(f32)
    sum_s[...] = total
    for j, piece in enumerate(pieces):
        piece[...] = sum_s[j * CAP : (j + 1) * CAP, :].astype(bf16)


def join_kernel(*refs):
    parts, out_ref, sum_s = by_partner(refs[:-2]), refs[-2], refs[-1]
    for j, part in enumerate(parts):
        sum_s[j * CAP : (j + 1) * CAP, :] = part[...].astype(f32)
    out_ref[...] = sum_s[...].astype(bf16)


def prep_kernel(
    cot_ref, w_ref, wq_ref, wk_ref, wv_ref, low_ref, place_ref, attt_ref,
    gh_ref, stack_ref, k_ref, qt_ref, vt_ref, wout_ref, qsel_ref, ght_s, mcot_s,
):
    count, tokens, width = gh_ref.shape
    for i in range(0, tokens, 256):
        rows = pl.ds(i, 256)
        where = place_ref[rows, :].astype(f32)
        free = 1.0 - jnp.sum(where, axis=-1, keepdims=True)
        mcot_s[rows, :] = (cot_ref[rows, :].astype(f32) * free).astype(bf16)
        slots = jnp.transpose(where).astype(bf16)
        for h in range(count):
            stack_ref[h, width:, rows] = slots
    gh = dot_nt(mcot_s[...], w_ref[...]).astype(bf16)
    ght_s[...] = dot_nt(w_ref[...], mcot_s[...]).astype(bf16)
    k = dot_nt(low_ref[...], wk_ref[...]).astype(bf16)
    qt_ref[...] = dot_nt(wq_ref[...], low_ref[...]).astype(bf16) * bf16(width ** (-0.5))
    vt_ref[...] = dot_nt(wv_ref[...], low_ref[...]).astype(bf16)
    for h in range(count):
        cols = slice(h * width, (h + 1) * width)
        gh_ref[h] = gh[:, cols]
        k_ref[h] = k[:, cols]
        stack_ref[h, 0:width, :] = ght_s[cols, :]
    wout_ref[...] = dot(attt_ref[...], mcot_s[...])
    qsel_ref[...] = dot(qt_ref[...], place_ref[...]).astype(bf16)


def masked_back_kernel(
    gh_ref, stack_ref, k_ref, qt_ref, vt_ref, att_ref, prob_ref,
    dq_ref, dkt_ref, dvt_ref, offs_ref, psel_ref, acc_s, score_s, *, h,
):
    tokens, width = dq_ref.shape
    acc_s[...] = jnp.zeros_like(acc_s)
    cols = slice(h * width, (h + 1) * width)
    for i in range(0, tokens, 2 * BLOCK):
        rows = pl.ds(i, 2 * BLOCK)
        gh = gh_ref[h, rows, :]
        delta = jnp.sum(gh.astype(f32) * att_ref[h, rows, :].astype(f32), axis=-1, keepdims=True)
        grads = dot(gh, vt_ref[cols, :]) - delta
        for j in range(2):
            start = i + j * BLOCK
            first = tokens - BLOCK - start
            here = pl.ds(start, BLOCK)
            score = prob_ref[h, here, :].astype(f32) * grads[j * BLOCK : (j + 1) * BLOCK]
            acc_s[:, first : first + tokens] += score
            score_s[here, :] = score.astype(bf16)
    dq_ref[...] = dot(score_s[...], k_ref[h]) * (width ** (-0.5))
    dkt_ref[...] = dot(qt_ref[cols, :], score_s[...])
    both = dot(stack_ref[h], prob_ref[h])
    dvt_ref[...] = both[:width]
    psel_ref[...] = both[width:].astype(bf16)
    offs_ref[...] = diagonals(acc_s[...])


def diagonals(acc):
    span = acc.shape[1]
    rows = acc.shape[0] // 2
    while rows >= 8:
        acc = acc[:rows] + pltpu.roll(acc[rows:], span - rows, 1)
        rows //= 2
    total = acc[0:1]
    for r in range(1, 8):
        total = total + pltpu.roll(acc[r : r + 1], span - r, 1)
    return jnp.broadcast_to(pltpu.roll(total, BLOCK - 1, 1), (8, span))


def slot_back_kernel(*refs, heads):
    parts = refs[:heads]
    (up_ref, normed_ref, hidden_ref, probs_ref, router_ref, gain_ref, w_ref, att_ref,
     wout0_ref) = refs[heads : heads + 9]
    (dv_ref, comb_ref, small_ref, wout_ref, gh_ref, ght_ref, delta_ref, ret_s, wide_s
     ) = refs[heads + 9 :]
    head, shard = lax.axis_index("head"), lax.axis_index("seq")
    ret_s[...] = jnp.zeros_like(ret_s)
    for d in range(heads):
        part = parts[d][...].astype(f32)
        for j in range(part.shape[0] // CAP):
            first = pl.multiple_of((shard ^ j) * SLOT, SLOT)
            ret_s[head ^ d, pl.ds(first, CAP), :] = part[j * CAP : (j + 1) * CAP]
    back = [ret_s[k] for k in range(heads)]
    combined = jnp.concatenate(back[: heads // 2], axis=1)
    grad_buf = jnp.concatenate(back[heads // 2 :], axis=1)
    up = up_ref[...].astype(f32)
    hidden, normed, probs, gain = hidden_ref[...], normed_ref[...], probs_ref[...], gain_ref[...]
    chosen = chosen_of(probs.shape)
    gate = jnp.sum(jnp.where(chosen, probs, 0.0), axis=-1, keepdims=True)
    comb_ref[...] = gate * combined
    gate_grad = jnp.sum(up * combined, axis=-1, keepdims=True)
    marked = jnp.where(chosen, gate_grad, 0.0)
    logit_grad = probs * (marked - jnp.sum(marked * probs, axis=-1, keepdims=True))
    experts = probs.shape[1]
    grad = grad_buf + jnp.dot(
        logit_grad, router_ref[...], precision=highest, preferred_element_type=f32
    )
    inverse = lax.rsqrt(jnp.mean(hidden * hidden, axis=-1, keepdims=True) + EPS)
    scaled = grad * gain
    inner_sum = jnp.mean(scaled * hidden, axis=-1, keepdims=True)
    dv = inverse * scaled - hidden * (inverse * inverse * inverse * inner_sum)
    dv_ref[...] = dv
    small_ref[...] = jnp.zeros_like(small_ref)
    small_ref[0:1, :] = jnp.sum(grad * hidden * inverse, axis=0, keepdims=True)
    small_ref[8 : 8 + experts, :] = dot_tn(logit_grad, normed, highest)
    grad_low = (up + dv).astype(bf16)
    half = att_ref.shape[0]
    inner = w_ref.shape[0]
    att = jnp.concatenate(
        [att_ref[:, 0:inner].astype(f32), att_ref[:, inner : 2 * inner].astype(f32)], axis=0
    )
    att = widen(att, wide_s)
    wout_ref[...] = wout0_ref[...] + dot_tn(att.astype(bf16), grad_low)
    gh = dot_nt(grad_low, w_ref[...])
    gh_low = gh.astype(bf16)
    count = gh_ref.shape[0]
    each = inner // count
    ght_ref[...] = dot_nt(w_ref[...], grad_low).astype(bf16)
    for h in range(count):
        cols = slice(h * each, (h + 1) * each)
        gh_ref[h] = gh_low[:, cols]
        delta_ref[h] = jnp.sum(
            gh_low[:, cols].astype(f32) * att[:, cols], axis=-1, keepdims=True
        )


def sparse_back_kernel(
    gh_ref, ght_ref, delta_ref, vt_ref, k_ref, qsel_ref,
    place_ref, wq_ref, wk_ref, wv_ref, low_ref, gain_ref, small_ref, wout_ref, *refs, heads,
):
    per_head, refs = refs[: 4 * gh_ref.shape[0]], refs[4 * gh_ref.shape[0] :]
    psels, dq0s, dkt0s, dvt0s = (per_head[i :: 4] for i in range(4))
    chunks = refs[:5]
    (score_ref, send_ref, keep_ref, out_ref,
     dq_s, q_low, k_low, v_low, kt_s, vt_s, all_s) = refs[5:]
    head = lax.axis_index("head")
    count, rows, width = gh_ref.shape
    tokens = vt_ref.shape[1]
    inner = count * width
    for h in range(count):
        cols = slice(h * width, (h + 1) * width)
        grad = dot(gh_ref[h], vt_ref[cols, :])
        prob = psels[h][...]
        score = (prob.astype(f32) * (grad - delta_ref[h])).astype(bf16)
        score_ref[h] = score
        dq_s[:, cols] = dot(score, k_ref[h]) * (width ** (-0.5))
        dkt = dkt0s[h][...] + dot(qsel_ref[cols, :], score)
        dvt = dvt0s[h][...] + dot(ght_ref[cols, :], prob)
        kt_s[cols, :] = dkt.astype(bf16)
        vt_s[cols, :] = dvt.astype(bf16)
        k_low[:, cols] = jnp.transpose(dkt).astype(bf16)
        v_low[:, cols] = jnp.transpose(dvt).astype(bf16)
    spread = dot(place_ref[...], dq_s[...].astype(bf16))
    for h in range(count):
        cols = slice(h * width, (h + 1) * width)
        q_low[:, cols] = (spread[:, cols] + dq0s[h][...]).astype(bf16)
    part = tokens // heads
    half = part // 2
    own, to_1, to_2, rest_1, rest_2 = chunks
    to_1[part:, :] = jnp.zeros((EXTRA, to_1.shape[1]), bf16)
    places = (
        ((own, 0), (own, half)),
        ((to_1, 0), (rest_1, 0)),
        ((rest_2, 0), (to_2, 0)),
        ((to_1, half), (to_2, half)),
    )
    for d in range(heads):
        mine = pl.ds(pl.multiple_of((head ^ d) * part, part), part)
        rows_part = (
            dot(q_low[mine, :], wq_ref[...])
            + dot(k_low[mine, :], wk_ref[...])
            + dot(v_low[mine, :], wv_ref[...])
        ).astype(bf16)
        for n, (ref, first) in enumerate(places[d]):
            ref[first : first + half, :] = rows_part[n * half : (n + 1) * half]
    low = low_ref[...]
    total = None
    grads = (dot_tn(q_low[...], low), dot(kt_s[...], low), dot(vt_s[...], low))
    for i, (grad, w) in enumerate(zip(grads, (wq_ref, wk_ref, wv_ref))):
        all_s[i * inner : (i + 1) * inner, :] = grad
        term = jnp.sum(grad * w[...].astype(f32), axis=0, keepdims=True)
        total = term if total is None else total + term
    all_s[3 * inner :, :] = wout_ref[...]
    out_ref[...] = small_ref[...]
    out_ref[1:2, :] = total / gain_ref[...]
    to_1[part : part + 1, :] = (total / gain_ref[...]).astype(bf16)
    split_rows(all_s, 1, send_ref, keep_ref)


def is_upper(bit):
    return (lax.axis_index("seq") & bit) != 0


def split_rows(all_s, bit, send_ref, keep_ref):
    half = send_ref.shape[0]
    low, high = all_s[0:half, :], all_s[half : 2 * half, :]
    keep_ref[...] = jnp.where(is_upper(bit), high, low)
    send_ref[...] = jnp.where(is_upper(bit), low, high).astype(bf16)


def halve_kernel(keep_ref, got_ref, *refs, bit):
    send_ref, out_ref, all_s = refs[-3:]
    if len(refs) > 3:
        rest_1, got_1, rest_2, got_2, small_ref, next_1, next_2 = refs[:-3]
        half = rest_1.shape[0]
        for rest, got, onward in ((rest_1, got_2, next_1), (rest_2, got_1, next_2)):
            got_rest = got[half : 2 * half, :].astype(f32)
            onward[0:half, :] = (rest[...].astype(f32) + got_rest).astype(bf16)
        mine = small_ref[1:2, :].astype(bf16).astype(f32)
        next_2[half:, :] = jnp.zeros((EXTRA, next_2.shape[1]), bf16)
        next_2[half : half + 1, :] = (mine + got_1[2 * half : 2 * half + 1, :].astype(f32)).astype(bf16)
    all_s[...] = keep_ref[...] + got_ref[...].astype(f32)
    split_rows(all_s, bit, send_ref, out_ref)


def join_rows(mine_ref, got_ref, all_s, bit, count):
    mine, got = mine_ref[...].astype(f32), got_ref[...].astype(f32)
    all_s[0:count, :] = jnp.where(is_upper(bit), got[:count], mine[:count])
    all_s[count : 2 * count, :] = jnp.where(is_upper(bit), mine[:count], got[:count])
    all_s[2 * count :, :] = mine[count:] + got[count:]


def pair_kernel(mine_ref, got_ref, *refs, bit, count):
    out_ref, all_s = refs[-2:]
    if len(refs) > 2:
        got_1, got_2, next_1, next_2 = refs[:-2]
        half = next_1.shape[0]
        next_2[...] = got_1[0:half, :]
        next_1[...] = got_2[half:, :]
    join_rows(mine_ref, got_ref, all_s, bit, count)
    out_ref[...] = all_s[...].astype(bf16)


def final_kernel(mine_ref, got_ref, *refs, bit, count):
    gain1_ref, gain2_ref, table_ref, router_ref, all_s = refs[-5:]
    outs = refs[:-5]
    join_rows(mine_ref, got_ref, all_s, bit, count)
    inner = outs[0].shape[0]
    for i, out in enumerate(outs):
        out[...] = all_s[i * inner : (i + 1) * inner, :]
    small = all_s[2 * count :, :]
    gain1_ref[...] = small[1, :]
    gain2_ref[...] = small[0, :]
    heads, buckets = table_ref.shape
    table_ref[...] = small[2 : 2 + heads, :buckets]
    router_ref[...] = small[8 : 8 + router_ref.shape[0], :]


def bias_grad_kernel(
    score_ref, place_ref, buckets_ref, small_ref, *refs, bucket_count
):
    count = score_ref.shape[0]
    offs, out_ref, acc_s, sums_s = refs[:count], *refs[count:]
    tokens = place_ref.shape[0]
    offsets = buckets_ref.shape[1]
    out_ref[...] = small_ref[...]
    bucket_hot = (iota((bucket_count, offsets), 0) == buckets_ref[...]).astype(f32)

    def one_head(h, carry):
        acc_s[...] = jnp.zeros_like(acc_s)
        for i in range(0, tokens, BLOCK):
            first = tokens - BLOCK - i
            acc_s[:, first : first + tokens] += dot(place_ref[i : i + BLOCK, :], score_ref[h])
        sums_s[h] = diagonals(acc_s[...])
        return carry

    lax.fori_loop(0, count, one_head, 0)
    for h in range(count):
        sums = sums_s[h] + offs[h][...]
        out_ref[2 + h : 3 + h, :bucket_count] = dot_nt(sums[:, :offsets], bucket_hot, highest)[0:1]


def hidden_kernel(*refs, heads):
    att_parts, w_ref, x_ref, out_ref, att_s = refs[:heads], *refs[heads:]
    head = lax.axis_index("head")
    tokens = x_ref.shape[0]
    inner = att_parts[0].shape[0]
    for d in range(heads):
        mine = pl.ds(pl.multiple_of((head ^ d) * inner, inner), inner)
        att_s[mine, :] = att_parts[d][...]

    def block(i, carry):
        rows = pl.ds(pl.multiple_of(i * 256, 256), 256)
        out_ref[rows, :] = x_ref[rows, :].astype(f32) + dot_tn(att_s[:, rows], w_ref[...])
        return carry

    lax.fori_loop(0, tokens // 256, block, 0)


def output_kernel(hidden_ref, place_ref, comb_ref, out_ref):
    high, rest = split_two(comb_ref[...])

    def block(i, carry):
        rows = pl.ds(pl.multiple_of(i * 256, 256), 256)
        where = place_ref[rows, :]
        out_ref[rows, :] = hidden_ref[rows, :] + (dot(where, high) + dot(where, rest))
        return carry

    lax.fori_loop(0, hidden_ref.shape[0] // 256, block, 0)


def first_norm_kernel(
    own, got_1, got_2, last_1, last_2, next_2, small_ref,
    x_ref, cot_ref, place_ref, dv_ref, gain_ref, keep_ref, got_ref, out_ref, sum_ref,
):
    half = last_1.shape[0]
    high, rest = split_two(dv_ref[...])
    for first, near, far in ((0, got_1, last_2), (half, got_2, last_1)):
        rows = pl.ds(first, half)
        grad = own[rows, :].astype(f32) + near[0:half, :].astype(f32)
        grad = grad + far[0:half, :].astype(f32)
        x = x_ref[rows, :].astype(f32)
        inverse = lax.rsqrt(jnp.mean(x * x, axis=-1, keepdims=True) + EPS)
        scaled = grad * gain_ref[...]
        inner_sum = jnp.mean(scaled * x, axis=-1, keepdims=True)
        where = place_ref[rows, :]
        hidden_grad = cot_ref[rows, :].astype(f32) + (dot(where, high) + dot(where, rest))
        out_ref[rows, :] = (
            hidden_grad + inverse * scaled - x * (inverse * inverse * inverse * inner_sum)
        ).astype(bf16)
    count = keep_ref.shape[0]
    sum_ref[0:count, :] = (keep_ref[...] + got_ref[...].astype(f32)).astype(bf16)
    gain1 = next_2[half:, :].astype(f32)[0:1] + last_2[half:, :].astype(f32)[0:1]
    small = small_ref[...]
    sum_ref[count:, :] = jnp.where(iota(small.shape, 0) == 1, gain1, small).astype(bf16)


def spread_near_kernel(own, got_1, got_2, out_ref, token, wide_s, sems):
    head = lax.axis_index("head")
    part = own.shape[0]
    copies = []
    for d, piece in enumerate((own, got_1, got_2)):
        wide_s[d] = piece[...].astype(f32)
        mine = pl.ds(pl.multiple_of((head ^ d) * part, part), part)
        copies.append(pltpu.make_async_copy(wide_s.at[d], out_ref.at[mine], sems.at[d]))
        copies[-1].start()
    token[...] = jnp.zeros_like(token)
    for copy in copies:
        copy.wait()


def spread_far_kernel(last_1, last_2, given, out_ref, wide_s, sem):
    head = lax.axis_index("head")
    half = last_1.shape[0]
    wide_s[0:half, :] = last_2[...].astype(f32)
    wide_s[half:, :] = last_1[...].astype(f32)
    mine = pl.ds(pl.multiple_of((head ^ 3) * 2 * half, 2 * half), 2 * half)
    copy = pltpu.make_async_copy(wide_s, out_ref.at[mine], sem)
    copy.start()
    copy.wait()


def swap(x, axis, d):
    size = lax.axis_size(axis)
    return lax.ppermute(x, axis, [(i, i ^ d) for i in range(size)])


def share(x, axis):
    return [x] + [swap(x, axis, d) for d in range(1, lax.axis_size(axis))]


def trade(pieces, axis):
    return lax.all_to_all(pieces, axis, split_axis=0, concat_axis=0, tiled=True)


def swap_all(pieces, axis):
    return [pieces[0]] + [swap(pieces[d], axis, d) for d in range(1, len(pieces))]


def bits_of(axis):
    return [b for b in (1 << i for i in range(16)) if b < lax.axis_size(axis)]


def halve(send, keep, bit, after, onward=()):
    rows, width = keep.shape
    outs = []
    if onward:
        half = onward[0].shape[0]
        outs = [shape_of(half, width, bf16), shape_of(half + EXTRA, width, bf16)]
    return call(
        partial(halve_kernel, bit=bit),
        outs + [shape_of(rows // 2, width, bf16), shape_of(rows // 2, width, f32)],
        (keep, swap(send, "seq", bit // 2)) + tuple(onward),
        scratch=[pltpu.VMEM((rows, width), f32)],
        name="halve",
        after=after,
        token=True,
    )


def pair(now, small_rows, bit, after, onward=()):
    rows, width = now.shape
    count = rows - small_rows
    outs = [shape_of(onward[0].shape[0] // 2, width, bf16)] * 2 if onward else []
    return call(
        partial(pair_kernel, bit=bit, count=count),
        outs + [shape_of(rows + count, width, bf16)],
        (now, swap(now, "seq", bit)) + tuple(onward),
        scratch=[pltpu.VMEM((rows + count, width), f32)],
        name="pair",
        after=after,
        token=True,
    )


def on_device(
    layer_input, cotangent, norm1_gain, w_query, w_key, w_value, w_attn_out, bias_table,
    norm2_gain, w_router, w_expert_in, w_expert_out, expert_ids, slot_ids, buckets,
):
    tokens, width = layer_input.shape
    shards = lax.axis_size("seq")
    heads = lax.axis_size("head")
    bucket_count, count = bias_table.shape
    inner = w_query.shape[1]
    each = inner // count
    experts = w_router.shape[1]
    rows, filled = experts * SLOT, experts * CAP
    hidden_units = w_expert_in.shape[2]
    part = tokens // heads
    split = 2 * width // heads
    span = 2 * tokens
    params = pltpu.CompilerParams(vmem_limit_bytes=VMEM_LIMIT if rows <= 256 else VMEM_ALL)

    ids = expert_ids.reshape(1, tokens)
    slots = slot_ids.reshape(1, tokens)
    bucket_row = buckets.reshape(1, -1)
    wq_t, wk_t, wv_t = jnp.transpose(w_query), jnp.transpose(w_key), jnp.transpose(w_value)
    router_t, table_t = jnp.transpose(w_router), jnp.transpose(bias_table)
    w_in = w_expert_in.reshape(width, hidden_units)
    w_out = w_expert_out.reshape(hidden_units, width)

    w_mix = share(w_attn_out, "head")

    low, prob, att, att_t, att_sel = pl.pallas_call(
        attend_kernel,
        out_shape=(
            shape_of(tokens, width, bf16),
            jax.ShapeDtypeStruct((count, tokens, tokens), bf16),
            jax.ShapeDtypeStruct((count, tokens, each), bf16),
            shape_of(inner, tokens, bf16),
            shape_of(filled // 2, 2 * inner, bf16),
        ),
        in_specs=[spec(pltpu.HBM)] * 9,
        out_specs=(spec(pltpu.VMEM),) * 5,
        scratch_shapes=[
            pltpu.VMEM((count, tokens, each), bf16),
            pltpu.VMEM((inner, tokens), bf16),
            pltpu.VMEM((count, tokens, each), bf16),
            pltpu.VMEM((8, span), f32),
            pltpu.VMEM((2, BLOCK, span), f32),
            pltpu.VMEM((filled, tokens), bf16),
            pltpu.VMEM((2, 2 * BLOCK, tokens), f32),
            pltpu.VMEM((tokens, width), bf16),
            pltpu.VMEM((width,), f32),
            pltpu.VMEM((inner, width), bf16),
            pltpu.VMEM((inner, width), bf16),
            pltpu.VMEM((inner, width), bf16),
            pltpu.VMEM((count, bucket_count), f32),
            pltpu.VMEM((1, span - 1), jnp.int32),
            pltpu.VMEM((1, tokens), jnp.int32),
            pltpu.VMEM((1, tokens), jnp.int32),
            pltpu.SemaphoreType.DMA((9,)),
        ],
        compiler_params=params,
        cost_estimate=NO_COST,
        name="attend",
    )(
        *(
            pltpu.with_memory_space_constraint(a, pltpu.HBM)
            for a in (layer_input, norm1_gain, wq_t, wk_t, wv_t, table_t, bucket_row, ids, slots)
        )
    )

    (att_sel,) = call(
        pass_kernel,
        [shape_of(filled // 2, 2 * inner, bf16)],
        (att_sel,),
        name="pass",
        after=(w_mix[1],),
    )
    sel_parts = share(att_sel, "head")
    sel_in, sel_up, place, place_c, x_c, cot_c, w_full = call(
        partial(place_kernel, heads=heads),
        [
            shape_of(rows, width, bf16),
            shape_of(rows, width, bf16),
            shape_of(tokens, rows, bf16),
            shape_of(part, rows, bf16),
            shape_of(part, width, bf16),
            shape_of(part, width, bf16),
            shape_of(heads * inner, width, bf16),
        ],
        (layer_input, cotangent, ids, slots) + tuple(w_mix),
        scratch=[pltpu.VMEM((tokens, rows), f32)],
        moved=12 * 2**20,
        name="place",
        after=(att_sel,),
    )
    routed = call(
        partial(route_kernel, shards=shards, heads=heads),
        [
            shape_of(rows, width, f32),
            shape_of(rows, width, f32),
            shape_of(rows, experts, f32),
            shape_of(inner, tokens, bf16),
        ]
        + [shape_of(TALL, packed_width(width), bf16)] * shards,
        tuple(sel_parts) + (w_full, sel_in, sel_up, norm2_gain, router_t, att_t),
        scratch=[
            pltpu.VMEM((heads, filled, inner), bf16),
            pltpu.VMEM((rows, 2 * width), f32),
            pltpu.VMEM((rows, width), f32),
            pltpu.VMEM((shards * TALL, packed_width(width)), f32),
        ],
        name="route",
    )
    hidden_sel, normed_sel, probs, att_on = routed[:4]
    pay_parts = swap_all(routed[4:], "seq")
    att_parts = [att_t] + [swap(att_on, "head", d) for d in range(1, heads - 1)]

    def masked_back(h, after):
        return call(
            partial(masked_back_kernel, h=h),
            [
                shape_of(tokens, each, f32),
                shape_of(each, tokens, f32),
                shape_of(each, tokens, f32),
                shape_of(8, span, f32),
                shape_of(rows, tokens, bf16),
            ],
            (gh, stack, k_rows, q_t, v_t, att, prob),
            scratch=[pltpu.VMEM((BLOCK, span), f32), pltpu.VMEM((tokens, tokens), bf16)],
            name="masked_back",
            after=after,
            moved=11 * 2**20,
            token=True,
        )

    done = call(
        partial(expert_kernel, shards=shards, heads=heads),
        [shape_of(filled, split, bf16)] * heads
        + [
            shape_of(rows, width, bf16),
            shape_of(rows, hidden_units, bf16),
            shape_of(rows, hidden_units, bf16),
            shape_of(rows, width, bf16),
        ],
        tuple(pay_parts[d] for d in far_first(shards)) + (w_in, w_out),
        scratch=[
            pltpu.VMEM((rows, 2 * width), f32),
            pltpu.VMEM((rows, 1), f32),
            pltpu.VMEM((heads, filled, split), f32),
        ],
        name="expert",
        after=tuple(att_parts[1:]),
        token=True,
    )
    x_rows, act, pre_low, out_low, token = done[heads:]
    gh, stack, k_rows, q_t, v_t, wout0, q_sel, token = call(
        prep_kernel,
        [
            jax.ShapeDtypeStruct((count, tokens, each), bf16),
            jax.ShapeDtypeStruct((count, each + rows, tokens), bf16),
            jax.ShapeDtypeStruct((count, tokens, each), bf16),
            shape_of(inner, tokens, bf16),
            shape_of(inner, tokens, bf16),
            shape_of(inner, width, f32),
            shape_of(inner, rows, bf16),
        ],
        (cotangent, w_attn_out, wq_t, wk_t, wv_t, low, place, att_t),
        scratch=[pltpu.VMEM((inner, tokens), bf16), pltpu.VMEM((tokens, width), bf16)],
        name="prep",
        after=(token,),
        moved=8 * 2**20,
        token=True,
    )

    masked = []
    for h in range(count - 2):
        masked.append(masked_back(h, (token,)))
        token = masked[-1][-1]
    returned = call(
        partial(sum_kernel, heads=heads),
        [shape_of(inner, tokens, bf16)] + [shape_of(CAP, split, bf16)] * shards,
        [att_t] + swap_all(done[:heads], "head"),
        scratch=[pltpu.VMEM((filled, split), f32)],
        name="sum",
        after=(token,),
        token=True,
    )
    masked.append(masked_back(count - 2, (returned[-1],)))
    att_parts.append(swap(returned[0], "head", heads - 1))
    answers = swap_all(returned[1:-1], "seq")
    joined, token = call(
        join_kernel,
        [shape_of(filled, split, bf16)],
        [answers[d] for d in far_first(shards)],
        scratch=[pltpu.VMEM((filled, split), f32)],
        name="join",
        after=(masked[-1][-1], att_parts[-1]),
        token=True,
    )
    masked.append(masked_back(count - 1, (token,)))
    full_parts = share(joined, "head")

    small_rows = 8 + -(-experts // 8) * 8
    dv_sel, comb_sel, small, wout_part, gh_sel, ght_sel, delta_sel = call(
        partial(slot_back_kernel, heads=heads),
        [
            shape_of(rows, width, f32),
            shape_of(rows, width, f32),
            shape_of(small_rows, width, f32),
            shape_of(inner, width, f32),
            jax.ShapeDtypeStruct((count, rows, each), bf16),
            shape_of(inner, rows, bf16),
            jax.ShapeDtypeStruct((count, rows, 1), f32),
        ],
        tuple(full_parts)
        + (sel_up, normed_sel, hidden_sel, probs, router_t, norm2_gain)
        + (w_attn_out, att_sel, wout0),
        scratch=[pltpu.VMEM((heads, rows, split), f32), pltpu.VMEM((rows, inner), f32)],
        name="slot_back",
        after=(masked[-1][-1],),
    )

    back = call(
        partial(sparse_back_kernel, heads=heads),
        [shape_of(part, width, bf16), shape_of(part + EXTRA, width, bf16)]
        + [shape_of(part, width, bf16)]
        + [shape_of(part // 2, width, bf16)] * 2
        + [
            jax.ShapeDtypeStruct((count, rows, tokens), bf16),
            shape_of(2 * inner, width, bf16),
            shape_of(2 * inner, width, f32),
            shape_of(small_rows, width, f32),
        ],
        (gh_sel, ght_sel, delta_sel, v_t, k_rows, q_sel, place)
        + (wq_t, wk_t, wv_t, low, norm1_gain, small, wout_part)
        + tuple(a for m in masked for a in (m[4], m[0], m[1], m[2])),
        scratch=[
            pltpu.VMEM((rows, inner), f32),
            pltpu.VMEM((tokens, inner), bf16),
            pltpu.VMEM((tokens, inner), bf16),
            pltpu.VMEM((tokens, inner), bf16),
            pltpu.VMEM((inner, tokens), bf16),
            pltpu.VMEM((inner, tokens), bf16),
            pltpu.VMEM((4 * inner, width), f32),
        ],
        name="sparse_back",
    )
    score_sel, send, keep, small = back[5:]
    own, to_1, to_2, rest_1, rest_2 = back[:5]
    got_1, got_2 = swap(to_1, "head", 1), swap(to_2, "head", 2)

    bits = bits_of("seq")
    send, keep, token = halve(send, keep, bits[1], ())
    small_part = small
    small, token = call(
        partial(bias_grad_kernel, bucket_count=bucket_count),
        [shape_of(small_rows, width, f32)],
        (score_sel, place, bucket_row, small) + tuple(m[3] for m in masked),
        scratch=[pltpu.VMEM((BLOCK, span), f32), pltpu.VMEM((count, 8, span), f32)],
        name="bias_grad",
        after=(token,),
        moved=16 * 2**20,
        token=True,
    )
    next_1, next_2, send, keep, token = halve(
        send, keep, bits[2], (token,), (rest_1, got_1, rest_2, got_2, small_part)
    )
    last_1, last_2 = swap(next_1, "head", 1), swap(next_2, "head", 2)
    w_in_grad, w_out_grad, token = call(
        expert_grad_kernel,
        [
            jax.ShapeDtypeStruct(w_expert_in.shape, f32),
            jax.ShapeDtypeStruct(w_expert_out.shape, f32),
        ],
        (x_rows, pre_low, act, out_low),
        name="expert_grad",
        after=(token,),
        moved=10 * 2**20,
        token=True,
    )
    hidden, token = call(
        partial(hidden_kernel, heads=heads),
        [shape_of(tokens, width, f32)],
        tuple(att_parts) + (w_full, layer_input),
        scratch=[pltpu.VMEM((heads * inner, tokens), bf16)],
        name="hidden",
        after=(token,),
        moved=6 * 2**20,
        token=True,
    )
    for bit in bits[3:]:
        send, keep, token = halve(send, keep, bit, (token,))

    grad_part, weights, token = call(
        first_norm_kernel,
        [shape_of(part, width, bf16), shape_of(keep.shape[0] + small_rows, width, bf16)],
        (own, got_1, got_2, last_1, last_2, next_2, small)
        + (x_c, cot_c, place_c, dv_sel, norm1_gain)
        + (keep, swap(send, "seq", bits[-1])),
        name="first_norm",
        after=(token,),
        token=True,
    )
    grad_1, grad_2 = swap(grad_part, "head", 1), swap(grad_part, "head", 2)
    layer_output, token = call(
        output_kernel,
        [shape_of(tokens, width, f32)],
        (hidden, place, comb_sel),
        name="output",
        after=(token,),
        moved=10 * 2**20,
        token=True,
    )
    for bit in reversed(bits[3:]):
        weights, token = pair(weights, small_rows, bit, (token,))
    next_1, next_2, weights, token = pair(
        weights, small_rows, bits[2], (token,), (grad_1, grad_2)
    )
    grad_3 = (swap(next_1, "head", 1), swap(next_2, "head", 2))
    near, token = pl.pallas_call(
        spread_near_kernel,
        out_shape=(shape_of(tokens, width, f32), shape_of(8, 128, f32)),
        in_specs=[spec(pltpu.VMEM)] * 3,
        out_specs=(spec(pltpu.HBM), spec(pltpu.VMEM)),
        scratch_shapes=[pltpu.VMEM((3, part, width), f32), pltpu.SemaphoreType.DMA((3,))],
        compiler_params=params,
        cost_estimate=pl.CostEstimate(flops=1, bytes_accessed=5 * 2**20, transcendentals=0),
        name="spread_near",
    )(grad_part, grad_1, grad_2)
    weights, token = pair(weights, small_rows, bits[1], grad_3 + (token,))
    last = call(
        partial(final_kernel, bit=bits[0], count=2 * inner),
        [shape_of(inner, width, f32)] * 4
        + [
            jax.ShapeDtypeStruct((width,), f32),
            jax.ShapeDtypeStruct((width,), f32),
            shape_of(count, bucket_count, f32),
            shape_of(experts, width, f32),
        ],
        (weights, swap(weights, "seq", bits[0])),
        scratch=[pltpu.VMEM((4 * inner + small_rows, width), f32)],
        name="weights_out",
    )
    weight_sums = last[:4]
    gain1_sum, gain2_sum, table_sum, router_sum = last[4:]
    input_grad = pl.pallas_call(
        spread_far_kernel,
        out_shape=shape_of(tokens, width, f32),
        in_specs=[spec(pltpu.VMEM), spec(pltpu.VMEM), spec(pltpu.HBM)],
        out_specs=spec(pltpu.HBM),
        scratch_shapes=[pltpu.VMEM((part, width), f32), pltpu.SemaphoreType.DMA(())],
        input_output_aliases={2: 0},
        compiler_params=params,
        cost_estimate=NO_COST,
        name="spread_far",
    )(*grad_3, near)

    return (
        layer_output,
        input_grad,
        gain1_sum,
        jnp.transpose(weight_sums[0]),
        jnp.transpose(weight_sums[1]),
        jnp.transpose(weight_sums[2]),
        weight_sums[3],
        jnp.transpose(table_sum),
        gain2_sum,
        jnp.transpose(router_sum),
        w_in_grad,
        w_out_grad,
    )


def solution(mesh):
    return jax.shard_map(
        on_device,
        mesh=mesh,
        in_specs=(
            P("seq", None),
            P("seq", None),
            P(),
            P(None, "head"),
            P(None, "head"),
            P(None, "head"),
            P("head", None),
            P(None, "head"),
            P(),
            P(),
            P("seq", None, "head"),
            P("seq", "head", None),
            P("seq"),
            P("seq"),
            P(),
        ),
        out_specs=(
            P("seq", None),
            P("seq", None),
            P(),
            P(None, "head"),
            P(None, "head"),
            P(None, "head"),
            P("head", None),
            P(None, "head"),
            P(),
            P(),
            P("seq", None, "head"),
            P("seq", "head", None),
        ),
        check_vma=False,
    )
```

profile of v0, /device:TPU:0, one launch (start us, length us, event | category | flops | bytes accessed | tf_op | source)
XLA Modules:
  0.0 132.7 jit_solution(12464442294440568793)
XLA Ops:
  0.7 3.0 %collective-permute-start = (bf16[192,768]{1,0:T(8,128)(2,1)}, bf16[192,768]{1,0:T(8,128)(2,1)S(1)}, u32[]{:S(2)}, u32[]{:S(2)}) collective-permute-start(bf16[192,768]{1,0:T(8,128)(2,1)} %refs_10_.1), channel_id=1, source_target_pairs={{0,8},{8,0},{16,24},{24,16},{1,9},{9,1},{17,25},{25,17},{2,10},{10... | collective-permute-start | bytes 884744 | tf_op jit(solution)/shard_map/ppermute | solution.py:711
  3.7 1.5 %collective-permute-start.5 = (bf16[192,768]{1,0:T(8,128)(2,1)}, bf16[192,768]{1,0:T(8,128)(2,1)S(1)}, u32[]{:S(2)}, u32[]{:S(2)}) collective-permute-start(bf16[192,768]{1,0:T(8,128)(2,1)} %refs_10_.1), channel_id=1, source_target_pairs={{0,24},{8,16},{16,8},{24,0},{1,25},{9,17},{17,9},{25,1},{2,26},{10... | collective-permute-start | bytes 884744 | tf_op jit(solution)/shard_map/ppermute | solution.py:711
  5.2 11.3 %attend.1 = (bf16[1024,768]{1,0:T(8,128)(2,1)S(1)}, bf16[3,1024,1024]{2,1,0:T(8,128)(2,1)S(1)}, bf16[3,1024,64]{2,1,0:T(8,128)(2,1)S(1)}, bf16[192,1024]{1,0:T(8,128)(2,1)S(1)}, bf16[80,384]{1,0:T(8,128)(2,1)S(1)}) custom-call(bf16[1024,768]{1,0:T(8,128)(2,1)} %refs_5_.1, f32[768]{0:T(1024)} %refs_11_.3, bf16[192,768]{1,0:T(8,128)(2,1)} %bitcast.15, ...), custom_call_target="tpu_custom_call" | custom-call | flops 1 | bytes 1 | tf_op jit(solution)/shard_map/attend/pallas_call | solution.py:790
  16.6 3.0 %collective-permute-start.3 = (bf16[80,384]{1,0:T(8,128)(2,1)S(1)}, bf16[80,384]{1,0:T(8,128)(2,1)S(1)}, u32[]{:S(2)}, u32[]{:S(2)}) collective-permute-start(bf16[80,384]{1,0:T(8,128)(2,1)S(1)} %pass.1.refs_8_.refs_0_.refs_11_), channel_id=1, source_target_pairs={{0,24},{8,16},{16,8},{24,0},{1,25},{9,17},{17,9},{25,1},{2,26},{10... | collective-permute-start | bytes 184328 | tf_op jit(solution)/shard_map/ppermute | solution.py:711
  20.6 1.4 %copy-done.1 = bf16[1024,768]{1,0:T(8,128)(2,1)S(1)} copy-done((bf16[1024,768]{1,0:T(8,128)(2,1)S(1)}, bf16[1024,768]{1,0:T(8,128)(2,1)}, u32[]{:S(2)}) %copy-start.1) | copy-done | bytes 1572888
  22.0 1.1 place.1
  23.2 0.6 collective-permute-done.2.refs_2_
  24.3 1.7 %route.1 = (f32[192,768]{1,0:T(8,128)S(1)}, f32[192,768]{1,0:T(8,128)S(1)}, f32[192,8]{1,0:T(8,128)S(1)}, bf16[192,1024]{1,0:T(8,128)(2,1)S(1)}, bf16[16,2048]{1...) custom-call(bf16[80,384]{1,0:T(8,128)(2,1)S(1)} %pass.1.refs_8_.refs, ...), custom_call_target="tpu_custom_call" | custom-call | flops 1 | bytes 1 | tf_op jit(solution)/shard_map/route/pallas_call | solution.py:74
  26.0 1.6 %collective-permute-start.7 = (bf16[192,1024]{1,0:T(8,128)(2,1)S(1)}, bf16[192,1024]{1,0:T(8,128)(2,1)S(1)}, u32[]{:S(2)}, u32[]{:S(2)}) collective-permute-start(bf16[192,1024]{1,0:T(8,128)(2,1)S(1)} %get-tuple-element.138), channel_id=1, source_target_pairs={{0,16},{8,24},{16,0},{24,8},{1,17},{9,25},{17,1},{25,9},{2,18},{10... | collective-permute-start | bytes 1179656 | tf_op jit(solution)/shard_map/ppermute | solution.py:711
  27.6 0.5 collective-permute-start.6
  28.2 3.6 %collective-permute-start.8 = (bf16[16,2048]{1,0:T(8,128)(2,1)S(1)}, bf16[16,2048]{1,0:T(8,128)(2,1)S(1)}, u32[]{:S(2)}, u32[]{:S(2)}) collective-permute-start(bf16[16,2048]{1,0:T(8,128)(2,1)S(1)} %get-tuple-element.139), channel_id=1, source_target_pairs={{0,6},{1,7},{2,4},{3,5},{4,2},{5,3},{6,0},{7,1},{8,14},{9,15},{10,... | collective-permute-start | bytes 196616 | tf_op jit(solution)/shard_map/ppermute | solution.py:711
  31.8 2.6 %collective-permute-done.8.refs_0_ = bf16[16,2048]{1,0:T(8,128)(2,1)S(1)} collective-permute-done((bf16[16,2048]{1,0:T(8,128)(2,1)S(1)}, bf16[16,2048]{1,0:T(8,128)(2,1)S(1)}, u32[]{:S(2)}, u32[]{:S(2)}) %collective-permute-start.8) | collective-permute-done | bytes 65568 | tf_op jit(solution)/shard_map/ppermute | solution.py:711
  34.3 3.0 %collective-permute-done.9.refs_1_ = bf16[16,2048]{1,0:T(8,128)(2,1)S(1)} collective-permute-done((bf16[16,2048]{1,0:T(8,128)(2,1)S(1)}, bf16[16,2048]{1,0:T(8,128)(2,1)S(1)}, u32[]{:S(2)}, u32[]{:S(2)}) %collective-permute-start.9) | collective-permute-done | bytes 65568 | tf_op jit(solution)/shard_map/ppermute | solution.py:711
  37.3 2.4 %collective-permute-start.12 = (bf16[16,2048]{1,0:T(8,128)(2,1)S(1)}, bf16[16,2048]{1,0:T(8,128)(2,1)S(1)}, u32[]{:S(2)}, u32[]{:S(2)}) collective-permute-start(bf16[16,2048]{1,0:T(8,128)(2,1)S(1)} %get-tuple-element.143), channel_id=1, source_target_pairs={{0,2},{1,3},{2,0},{3,1},{4,6},{5,7},{6,4},{7,5},{8,10},{9,11},{10,... | collective-permute-start | bytes 196616 | tf_op jit(solution)/shard_map/ppermute | solution.py:711
  39.8 1.3 collective-permute-done.10.refs_2_
  41.1 1.6 %collective-permute-done.11.refs_3_ = bf16[16,2048]{1,0:T(8,128)(2,1)S(1)} collective-permute-done((bf16[16,2048]{1,0:T(8,128)(2,1)S(1)}, bf16[16,2048]{1,0:T(8,128)(2,1)S(1)}, u32[]{:S(2)}, u32[]{:S(2)}) %collective-permute-start.11) | collective-permute-done | bytes 65568 | tf_op jit(solution)/shard_map/ppermute | solution.py:711
  42.7 0.8 collective-permute-done.12.refs_4_
  43.5 1.7 %collective-permute-done.13.refs_5_ = bf16[16,2048]{1,0:T(8,128)(2,1)S(1)} collective-permute-done((bf16[16,2048]{1,0:T(8,128)(2,1)S(1)}, bf16[16,2048]{1,0:T(8,128)(2,1)S(1)}, u32[]{:S(2)}, u32[]{:S(2)}) %collective-permute-start.13) | collective-permute-done | bytes 65568 | tf_op jit(solution)/shard_map/ppermute | solution.py:711
  45.3 1.6 %expert.1 = (bf16[160,384]{1,0:T(8,128)(2,1)S(1)}, bf16[160,384]{1,0:T(8,128)(2,1)S(1)}, bf16[160,384]{1,0:T(8,128)(2,1)S(1)}, bf16[160,384]{1,0:T(8,128)(2,1)S(...) custom-call(bf16[16,2048]{1,0:T(8,128)(2,1)S(1)} %collective-permute, ...), custom_call_target="tpu_custom_call" | custom-call | flops 1 | bytes 1 | tf_op jit(solution)/shard_map/expert/pallas_call | solution.py:74
  46.9 1.6 %collective-permute-start.15 = (bf16[160,384]{1,0:T(8,128)(2,1)S(1)}, bf16[160,384]{1,0:T(8,128)(2,1)S(1)}, u32[]{:S(2)}, u32[]{:S(2)}) collective-permute-start(bf16[160,384]{1,0:T(8,128)(2,1)S(1)} %get-tuple-element.148), channel_id=1, source_target_pairs={{0,8},{8,0},{16,24},{24,16},{1,9},{9,1},{17,25},{25,17},{2,10},{10... | collective-permute-start | bytes 368648 | tf_op jit(solution)/shard_map/ppermute | solution.py:711
  49.0 1.5 %collective-permute-start.17 = (bf16[160,384]{1,0:T(8,128)(2,1)S(1)}, bf16[160,384]{1,0:T(8,128)(2,1)S(1)}, u32[]{:S(2)}, u32[]{:S(2)}) collective-permute-start(bf16[160,384]{1,0:T(8,128)(2,1)S(1)} %get-tuple-element.150), channel_id=1, source_target_pairs={{0,24},{8,16},{16,8},{24,0},{1,25},{9,17},{17,9},{25,1},{2,26},{10... | collective-permute-start | bytes 368648 | tf_op jit(solution)/shard_map/ppermute | solution.py:711
  50.5 2.9 %prep.1 = (bf16[3,1024,64]{2,1,0:T(8,128)(2,1)S(1)}, bf16[3,256,1024]{2,1,0:T(8,128)(2,1)S(1)}, bf16[3,1024,64]{2,1,0:T(8,128)(2,1)S(1)}, bf16[192,1024]{1,0:T(8...) custom-call(bf16[1024,768]{1,0:T(8,128)(2,1)S(1)} %copy-done.2, ...), custom_call_target="tpu_custom_call" | custom-call | flops 1 | bytes 8388608 | tf_op jit(solution)/shard_map/prep/pallas_call | solution.py:74
  53.4 2.5 %masked_back.3 = (f32[1024,64]{1,0:T(8,128)S(1)}, f32[64,1024]{1,0:T(8,128)S(1)}, f32[64,1024]{1,0:T(8,128)S(1)}, f32[8,2048]{1,0:T(8,128)S(1)}, bf16[192,1024]{1,0:T(8,128)(2,1)S(1)}, /*index=5*/f32[8,128]{1,0:T(8,128)S(1)}) custom-call(bf16[3,1024,64]{2,1,0:T(8,128)(2,1)S(1)} %get-tuple-element.154.refs_0_, ...), custom_call_target="tpu_custom_call" | custom-call | flops 1 | bytes 11534336 | tf_op jit(solution)/shard_map/masked_back/pallas_call | solution.py:74
  56.3 1.4 %collective-permute-start.18 = (bf16[192,1024]{1,0:T(8,128)(2,1)S(1)}, bf16[192,1024]{1,0:T(8,128)(2,1)S(1)}, u32[]{:S(2)}, u32[]{:S(2)}) collective-permute-start(bf16[192,1024]{1,0:T(8,128)(2,1)S(1)} %get-tuple-element.163), channel_id=1, source_target_pairs={{0,24},{8,16},{16,8},{24,0},{1,25},{9,17},{17,9},{25,1},{2,26},{10... | collective-permute-start | bytes 1179656 | tf_op jit(solution)/shard_map/ppermute | solution.py:711
  57.6 2.7 %collective-permute-start.19 = (bf16[20,384]{1,0:T(8,128)(2,1)S(1)}, bf16[20,384]{1,0:T(8,128)(2,1)S(1)}, u32[]{:S(2)}, u32[]{:S(2)}) collective-permute-start(bf16[20,384]{1,0:T(8,128)(2,1)S(1)} %get-tuple-element.168), channel_id=1, source_target_pairs={{0,6},{1,7},{2,4},{3,5},{4,2},{5,3},{6,0},{7,1},{8,14},{9,15},{10,... | collective-permute-start | bytes 46088 | tf_op jit(solution)/shard_map/ppermute | solution.py:711
  60.4 3.5 %collective-permute-start.22 = (bf16[20,384]{1,0:T(8,128)(2,1)S(1)}, bf16[20,384]{1,0:T(8,128)(2,1)S(1)}, u32[]{:S(2)}, u32[]{:S(2)}) collective-permute-start(bf16[20,384]{1,0:T(8,128)(2,1)S(1)} %get-tuple-element.171), channel_id=1, source_target_pairs={{0,5},{1,4},{2,7},{3,6},{4,1},{5,0},{6,3},{7,2},{8,13},{9,12},{10,... | collective-permute-start | bytes 46088 | tf_op jit(solution)/shard_map/ppermute | solution.py:711
  63.8 0.7 collective-permute-start.23
  64.5 0.9 collective-permute-done.20.refs_1_
  66.0 2.5 %masked_back.4 = (f32[1024,64]{1,0:T(8,128)S(1)}, f32[64,1024]{1,0:T(8,128)S(1)}, f32[64,1024]{1,0:T(8,128)S(1)}, f32[8,2048]{1,0:T(8,128)S(1)}, bf16[192,1024]{1,0:T(8,128)(2,1)S(1)}, /*index=5*/f32[8,128]{1,0:T(8,128)S(1)}) custom-call(bf16[3,1024,64]{2,1,0:T(8,128)(2,1)S(1)} %get-tuple-element.154.refs_0_, ...), custom_call_target="tpu_custom_call" | custom-call | flops 1 | bytes 11534336 | tf_op jit(solution)/shard_map/masked_back/pallas_call | solution.py:74
  68.7 1.6 %collective-permute-start.28 = (bf16[160,384]{1,0:T(8,128)(2,1)S(1)}, bf16[160,384]{1,0:T(8,128)(2,1)S(1)}, u32[]{:S(2)}, u32[]{:S(2)}) collective-permute-start(bf16[160,384]{1,0:T(8,128)(2,1)S(1)} %get-tuple-element.178.refs_0_), channel_id=1, source_target_pairs={{0,24},{8,16},{16,8},{24,0},{1,25},{9,17},{17,9},{25,1},{2,26},{10... | collective-permute-start | bytes 368648 | tf_op jit(solution)/shard_map/ppermute | solution.py:711
  70.3 0.5 collective-permute-start.27
  70.8 1.4 %collective-permute-start.26 = (bf16[160,384]{1,0:T(8,128)(2,1)S(1)}, bf16[160,384]{1,0:T(8,128)(2,1)S(1)}, u32[]{:S(2)}, u32[]{:S(2)}) collective-permute-start(bf16[160,384]{1,0:T(8,128)(2,1)S(1)} %get-tuple-element.178.refs_0_), channel_id=1, source_target_pairs={{0,8},{8,0},{16,24},{24,16},{1,9},{9,1},{17,25},{25,17},{2,10},{10... | collective-permute-start | bytes 368648 | tf_op jit(solution)/shard_map/ppermute | solution.py:711
  72.2 2.5 %masked_back.5 = (f32[1024,64]{1,0:T(8,128)S(1)}, f32[64,1024]{1,0:T(8,128)S(1)}, f32[64,1024]{1,0:T(8,128)S(1)}, f32[8,2048]{1,0:T(8,128)S(1)}, bf16[192,1024]{1,0:T(8,128)(2,1)S(1)}, /*index=5*/f32[8,128]{1,0:T(8,128)S(1)}) custom-call(bf16[3,1024,64]{2,1,0:T(8,128)(2,1)S(1)} %get-tuple-element.154.refs_0_, ...), custom_call_target="tpu_custom_call" | custom-call | flops 1 | bytes 11534336 | tf_op jit(solution)/shard_map/masked_back/pallas_call | solution.py:74
  74.8 1.0 collective-permute-done.28.refs_3_
  75.8 1.6 %collective-permute-done.27.refs_2_ = bf16[160,384]{1,0:T(8,128)(2,1)S(1)} collective-permute-done((bf16[160,384]{1,0:T(8,128)(2,1)S(1)}, bf16[160,384]{1,0:T(8,128)(2,1)S(1)}, u32[]{:S(2)}, u32[]{:S(2)}) %collective-permute-start.27) | collective-permute-done | bytes 122912 | tf_op jit(solution)/shard_map/ppermute | solution.py:711
  77.5 2.4 %slot_back.1 = (f32[192,768]{1,0:T(8,128)S(1)}, f32[192,768]{1,0:T(8,128)S(1)}, f32[16,768]{1,0:T(8,128)S(1)}, f32[192,768]{1,0:T(8,128)S(1)}, bf16[3,192,64]{2,...) custom-call(bf16[160,384]{1,0:T(8,128)(2,1)S(1)} %get-tuple-element.178.refs_0_, ...), custom_call_target="tpu_custom_call" | custom-call | flops 1 | bytes 1 | tf_op jit(solution)/shard_map/slot_back/pallas_call | solution.py:74
  80.0 4.1 %sparse_back.1 = (bf16[256,768]{1,0:T(8,128)(2,1)S(1)}, bf16[272,768]{1,0:T(8,128)(2,1)S(1)}, bf16[256,768]{1,0:T(8,128)(2,1)S(1)}, bf16[128,768]{1,0:T(8,128)(2...) custom-call(bf16[3,192,64]{2,1,0:T(8,128)(2,1)S(1)} %get-tuple-eleme, ...), custom_call_target="tpu_custom_call" | custom-call | flops 1 | bytes 1 | tf_op jit(solution)/shard_map/sparse_back/pallas_call | solution.py:74
  84.1 0.7 collective-permute-start.31
  84.9 1.5 %collective-permute-start.32 = (bf16[256,768]{1,0:T(8,128)(2,1)S(1)}, bf16[256,768]{1,0:T(8,128)(2,1)S(1)}, u32[]{:S(2)}, u32[]{:S(2)}) collective-permute-start(bf16[256,768]{1,0:T(8,128)(2,1)S(1)} %get-tuple-element.210), channel_id=1, source_target_pairs={{0,16},{8,24},{16,0},{24,8},{1,17},{9,25},{17,1},{25,9},{2,18},{10... | collective-permute-start | bytes 1179656 | tf_op jit(solution)/shard_map/ppermute | solution.py:711
  86.5 1.5 %collective-permute-start.30 = (bf16[192,768]{1,0:T(8,128)(2,1)S(1)}, bf16[192,768]{1,0:T(8,128)(2,1)S(1)}, u32[]{:S(2)}, u32[]{:S(2)}) collective-permute-start(bf16[192,768]{1,0:T(8,128)(2,1)S(1)} %get-tuple-element.206), channel_id=1, source_target_pairs={{0,2},{1,3},{2,0},{3,1},{4,6},{5,7},{6,4},{7,5},{8,10},{9,11},{10,... | collective-permute-start | bytes 884744 | tf_op jit(solution)/shard_map/ppermute | solution.py:711
  88.0 4.7 %bias_grad.1 = (f32[16,768]{1,0:T(8,128)S(1)}, f32[8,128]{1,0:T(8,128)S(1)}) custom-call(bf16[3,192,1024]{2,1,0:T(8,128)(2,1)S(1)} %get-tuple-element.212.refs_0_, bf16[1024,192]{1,0:T(8,128)(2,1)S(1)} %get-tuple-element.152.refs_6_.refs_1_, s32[1,2047]{1,0:T(1,128)S(1)} %bitcast.29, f32[16,768]{1,0:T(8,128)S(1)} %get-tuple-element.211.refs_3_.refs_6_, ...), custom_call_target="tpu_custom_call" | custom-call | flops 1 | bytes 16777216 | tf_op jit(solution)/shard_map/bias_grad/pallas_call | solution.py:74
  92.6 3.4 %collective-permute-done.32.refs_5_.refs_2_ = bf16[256,768]{1,0:T(8,128)(2,1)S(1)} collective-permute-done((bf16[256,768]{1,0:T(8,128)(2,1)S(1)}, bf16[256,768]{1,0:T(8,128)(2,1)S(1)}, u32[]{:S(2)}, u32[]{:S(2)}) %collective-permute-start.32) | collective-permute-done | bytes 393248 | tf_op jit(solution)/shard_map/ppermute | solution.py:711
  96.5 1.4 %collective-permute-start.34 = (bf16[144,768]{1,0:T(8,128)(2,1)S(1)}, bf16[144,768]{1,0:T(8,128)(2,1)S(1)}, u32[]{:S(2)}, u32[]{:S(2)}) collective-permute-start(bf16[144,768]{1,0:T(8,128)(2,1)S(1)} %get-tuple-element.224.refs_5_), channel_id=1, source_target_pairs={{0,16},{8,24},{16,0},{24,8},{1,17},{9,25},{17,1},{25,9},{2,18},{10... | collective-permute-start | bytes 663560 | tf_op jit(solution)/shard_map/ppermute | solution.py:711
  97.9 0.8 collective-permute-start.33
  98.7 1.6 %collective-permute-start.35 = (bf16[96,768]{1,0:T(8,128)(2,1)S(1)}, bf16[96,768]{1,0:T(8,128)(2,1)S(1)}, u32[]{:S(2)}, u32[]{:S(2)}) collective-permute-start(bf16[96,768]{1,0:T(8,128)(2,1)S(1)} %get-tuple-element.231), channel_id=1, source_target_pairs={{0,4},{1,5},{2,6},{3,7},{4,0},{5,1},{6,2},{7,3},{8,12},{9,13},{10,... | collective-permute-start | bytes 442376 | tf_op jit(solution)/shard_map/ppermute | solution.py:711
  100.3 2.8 %expert_grad.1 = (f32[1,768,768]{2,1,0:T(8,128)}, f32[1,768,768]{2,1,0:T(8,128)}, f32[8,128]{1,0:T(8,128)S(1)}) custom-call(bf16[192,768]{1,0:T(8,128)(2,1)S(1)} %get-tuple-element.164.refs_0_, bf16[192,768]{1,0:T(8,128)(2,1)S(1)} %get-tuple-element.165.refs_1_, bf16[192,768]{1,0:T(8,128)(2,1)S(1)} %get-tuple-element.166.refs_2_, ...), custom_call_target="tpu_custom_call" | custom-call | flops 1 | bytes 10485760 | tf_op jit(solution)/shard_map/expert_grad/pallas_call | solution.py:74
  103.0 2.3 %hidden.1 = (f32[1024,768]{1,0:T(8,128)S(1)}, f32[8,128]{1,0:T(8,128)S(1)}) custom-call(bf16[192,1024]{1,0:T(8,128)(2,1)S(1)} %get-tuple-element.133.refs_9_.refs_7_.refs_0_, bf16[192,1024]{1,0:T(8,128)(2,1)S(1)} %collective-permute-done.6.refs_10_.refs_1_, bf16[192,1024]{1,0:T(8,128)(2,1)S(1)} %collective-permute-done.7.refs_11_.refs_2_, ...), custom_call_target="tpu_custom_call" | custom-call | flops 1 | bytes 6291456 | tf_op jit(solution)/shard_map/hidden/pallas_call | solution.py:74
  105.4 2.2 %collective-permute-done.35.refs_13_ = bf16[96,768]{1,0:T(8,128)(2,1)S(1)} collective-permute-done((bf16[96,768]{1,0:T(8,128)(2,1)S(1)}, bf16[96,768]{1,0:T(8,128)(2,1)S(1)}, u32[]{:S(2)}, u32[]{:S(2)}) %collective-permute-start.35) | collective-permute-done | bytes 147488 | tf_op jit(solution)/shard_map/ppermute | solution.py:711
  107.6 0.7 first_norm.1
  108.3 0.9 collective-permute-start.38
  109.1 1.1 collective-permute-start.37
  110.3 3.2 %output.1 = (f32[1024,768]{1,0:T(8,128)}, f32[8,128]{1,0:T(8,128)S(1)}) custom-call(f32[1024,768]{1,0:T(8,128)S(1)} %get-tuple-element.220.refs_0_, bf16[1024,192]{1,0:T(8,128)(2,1)S(1)} %get-tuple-element.152.refs_6_.refs_1_, f32[192,768]{1,0:T(8,128)S(1)} %get-tuple-element.221.refs_2_, f32[8,128]{1,0:T(8,128)S(1)} %get-tuple-element.233.refs_3_), custom_call_target="tpu_custom_call" | custom-call | flops 1 | bytes 10485760 | tf_op jit(solution)/shard_map/output/pallas_call | solution.py:74
  113.5 6.0 %collective-permute-done.36.refs_1_ = bf16[112,768]{1,0:T(8,128)(2,1)S(1)} collective-permute-done((bf16[112,768]{1,0:T(8,128)(2,1)S(1)}, bf16[112,768]{1,0:T(8,128)(2,1)S(1)}, u32[]{:S(2)}, u32[]{:S(2)}) %collective-permute-start.36) | collective-permute-done | bytes 172064 | tf_op jit(solution)/shard_map/ppermute | solution.py:711
  119.5 0.6 pair.2
  120.1 1.2 collective-permute-start.39
  121.3 1.2 collective-permute-start.40
  122.5 1.5 %spread_near.1 = (f32[1024,768]{1,0:T(8,128)}, f32[8,128]{1,0:T(8,128)S(1)}) custom-call(bf16[256,768]{1,0:T(8,128)(2,1)S(1)} %get-tuple-element.236.own, bf16[256,768]{1,0:T(8,128)(2,1)S(1)} %collective-permute-done.37.refs_2_.got_1, bf16[256,768]{1,0:T(8,128)(2,1)S(1)} %collective-permute-done.38.refs_3_.got_2), custom_call_target="tpu_custom_call" | custom-call | flops 1 | bytes 5242880 | tf_op jit(solution)/shard_map/spread_near/pallas_call | solution.py:1079
  124.0 2.0 %collective-permute-done.39.last_1.refs_2_ = bf16[128,768]{1,0:T(8,128)(2,1)S(1)} collective-permute-done((bf16[128,768]{1,0:T(8,128)(2,1)S(1)}, bf16[128,768]{1,0:T(8,128)(2,1)S(1)}, u32[]{:S(2)}, u32[]{:S(2)}) %collective-permute-start.39) | collective-permute-done | bytes 196640 | tf_op jit(solution)/shard_map/ppermute | solution.py:711
  125.9 1.1 collective-permute-done.40.last_2.refs_3_
  127.0 1.5 %collective-permute-done.41.refs_1_ = bf16[208,768]{1,0:T(8,128)(2,1)S(1)} collective-permute-done((bf16[208,768]{1,0:T(8,128)(2,1)S(1)}, bf16[208,768]{1,0:T(8,128)(2,1)S(1)}, u32[]{:S(2)}, u32[]{:S(2)}) %collective-permute-start.41) | collective-permute-done | bytes 319520 | tf_op jit(solution)/shard_map/ppermute | solution.py:711
  128.6 0.6 pair.3
  129.2 0.9 spread_far.1
  130.1 1.1 collective-permute-done.42.refs_1_
  131.2 1.5 %weights_out.1 = (f32[192,768]{1,0:T(8,128)}, f32[192,768]{1,0:T(8,128)}, f32[192,768]{1,0:T(8,128)}, f32[192,768]{1,0:T(8,128)}, f32[768]{0:T(1024)}, /*index=5...) custom-call(bf16[400,768]{1,0:T(8,128)(2,1)S(1)} %get-tuple-element.243.refs_0_, ...), custom_call_target="tpu_custom_call" | custom-call | flops 1 | bytes 1 | tf_op jit(solution)/shard_map/weights_out/pallas_call | solution.py:74
  (77 shorter events, 4.0 us)
Async XLA Ops:
  0.6 19.9 %copy-start.3 = (bf16[192,768]{1,0:T(8,128)(2,1)S(1)}, bf16[192,768]{1,0:T(8,128)(2,1)}, u32[]{:S(2)}) copy-start(bf16[192,768]{1,0:T(8,128)(2,1)} %refs_10_.1) | copy-start | bytes 884740
  0.7 19.9 %copy-start = (bf16[1024,768]{1,0:T(8,128)(2,1)S(1)}, bf16[1024,768]{1,0:T(8,128)(2,1)}, u32[]{:S(2)}) copy-start(bf16[1024,768]{1,0:T(8,128)(2,1)} %refs_5_.1) | copy-start | bytes 4718596
  0.7 19.9 %copy-start.13 = (s32[1024]{0:T(1024)S(1)}, s32[1024]{0:T(1024)}, u32[]{:S(2)}) copy-start(s32[1024]{0:T(1024)} %param.28) | copy-start | bytes 12292
  0.7 19.9 %copy-start.12 = (s32[1024]{0:T(1024)S(1)}, s32[1024]{0:T(1024)}, u32[]{:S(2)}) copy-start(s32[1024]{0:T(1024)} %param.27) | copy-start | bytes 12292
  0.7 15.9 %collective-permute-start = (bf16[192,768]{1,0:T(8,128)(2,1)}, bf16[192,768]{1,0:T(8,128)(2,1)S(1)}, u32[]{:S(2)}, u32[]{:S(2)}) collective-permute-start(bf16[192,768]{1,0:T(8,128)(2,1)} %refs_10_.1), channel_id=1, source_target_pairs={{0,8},{8,0},{16,24},{24,16},{1,9},{9,1},{17,25},{25,17},{2,10},{10... | collective-permute-start | bytes 884744 | tf_op jit(solution)/shard_map/ppermute | solution.py:711
  3.7 16.5 %collective-permute-start.5 = (bf16[192,768]{1,0:T(8,128)(2,1)}, bf16[192,768]{1,0:T(8,128)(2,1)S(1)}, u32[]{:S(2)}, u32[]{:S(2)}) collective-permute-start(bf16[192,768]{1,0:T(8,128)(2,1)} %refs_10_.1), channel_id=1, source_target_pairs={{0,24},{8,16},{16,8},{24,0},{1,25},{9,17},{17,9},{25,1},{2,26},{10... | collective-permute-start | bytes 884744 | tf_op jit(solution)/shard_map/ppermute | solution.py:711
  5.2 15.4 %collective-permute-start.4 = (bf16[192,768]{1,0:T(8,128)(2,1)}, bf16[192,768]{1,0:T(8,128)(2,1)S(1)}, u32[]{:S(2)}, u32[]{:S(2)}) collective-permute-start(bf16[192,768]{1,0:T(8,128)(2,1)} %refs_10_.1), channel_id=1, source_target_pairs={{0,16},{8,24},{16,0},{24,8},{1,17},{9,25},{17,1},{25,9},{2,18},{10... | collective-permute-start | bytes 884744 | tf_op jit(solution)/shard_map/ppermute | solution.py:711
  16.6 7.7 %copy-start.9 = (f32[768,8]{0,1:T(8,128)S(1)}, f32[768,8]{0,1:T(8,128)}, u32[]{:S(2)}) copy-start(f32[768,8]{0,1:T(8,128)} %param.24) | copy-start | bytes 73732
  16.6 7.7 %copy-start.14 = (f32[768]{0:T(1024)S(1)}, f32[768]{0:T(1024)}, u32[]{:S(2)}) copy-start(f32[768]{0:T(1024)} %refs_9_.1) | copy-start | bytes 9220
  16.6 6.5 %collective-permute-start.3 = (bf16[80,384]{1,0:T(8,128)(2,1)S(1)}, bf16[80,384]{1,0:T(8,128)(2,1)S(1)}, u32[]{:S(2)}, u32[]{:S(2)}) collective-permute-start(bf16[80,384]{1,0:T(8,128)(2,1)S(1)} %pass.1.refs_8_.refs_0_.refs_11_), channel_id=1, source_target_pairs={{0,24},{8,16},{16,8},{24,0},{1,25},{9,17},{17,9},{25,1},{2,26},{10... | collective-permute-start | bytes 184328 | tf_op jit(solution)/shard_map/ppermute | solution.py:711
  19.6 4.2 %collective-permute-start.2 = (bf16[80,384]{1,0:T(8,128)(2,1)S(1)}, bf16[80,384]{1,0:T(8,128)(2,1)S(1)}, u32[]{:S(2)}, u32[]{:S(2)}) collective-permute-start(bf16[80,384]{1,0:T(8,128)(2,1)S(1)} %pass.1.refs_8_.refs_0_.refs_11_), channel_id=1, source_target_pairs={{0,16},{8,24},{16,0},{24,8},{1,17},{9,25},{17,1},{25,9},{2,18},{10... | collective-permute-start | bytes 184328 | tf_op jit(solution)/shard_map/ppermute | solution.py:711
  20.1 4.2 %collective-permute-start.1 = (bf16[80,384]{1,0:T(8,128)(2,1)S(1)}, bf16[80,384]{1,0:T(8,128)(2,1)S(1)}, u32[]{:S(2)}, u32[]{:S(2)}) collective-permute-start(bf16[80,384]{1,0:T(8,128)(2,1)S(1)} %pass.1.refs_8_.refs_0_.refs_11_), channel_id=1, source_target_pairs={{0,8},{8,0},{16,24},{24,16},{1,9},{9,1},{17,25},{25,17},{2,10},{10... | collective-permute-start | bytes 184328 | tf_op jit(solution)/shard_map/ppermute | solution.py:711
  20.6 1.4 %copy-start.1 = (bf16[1024,768]{1,0:T(8,128)(2,1)S(1)}, bf16[1024,768]{1,0:T(8,128)(2,1)}, u32[]{:S(2)}) copy-start(bf16[1024,768]{1,0:T(8,128)(2,1)} %refs_0_.5) | copy-start | bytes 4718596
  23.1 22.1 %copy-start.7 = (bf16[1,768,768]{2,1,0:T(8,128)(2,1)S(1)}, bf16[1,768,768]{2,1,0:T(8,128)(2,1)}, u32[]{:S(2)}) copy-start(bf16[1,768,768]{2,1,0:T(8,128)(2,1)} %param.25) | copy-start | bytes 3538948
  23.1 22.1 %copy-start.8 = (bf16[1,768,768]{2,1,0:T(8,128)(2,1)S(1)}, bf16[1,768,768]{2,1,0:T(8,128)(2,1)}, u32[]{:S(2)}) copy-start(bf16[1,768,768]{2,1,0:T(8,128)(2,1)} %param.26) | copy-start | bytes 3538948
  26.0 19.2 %collective-permute-start.7 = (bf16[192,1024]{1,0:T(8,128)(2,1)S(1)}, bf16[192,1024]{1,0:T(8,128)(2,1)S(1)}, u32[]{:S(2)}, u32[]{:S(2)}) collective-permute-start(bf16[192,1024]{1,0:T(8,128)(2,1)S(1)} %get-tuple-element.138), channel_id=1, source_target_pairs={{0,16},{8,24},{16,0},{24,8},{1,17},{9,25},{17,1},{25,9},{2,18},{10... | collective-permute-start | bytes 1179656 | tf_op jit(solution)/shard_map/ppermute | solution.py:711
  27.6 17.6 %collective-permute-start.6 = (bf16[192,1024]{1,0:T(8,128)(2,1)S(1)}, bf16[192,1024]{1,0:T(8,128)(2,1)S(1)}, u32[]{:S(2)}, u32[]{:S(2)}) collective-permute-start(bf16[192,1024]{1,0:T(8,128)(2,1)S(1)} %get-tuple-element.138), channel_id=1, source_target_pairs={{0,8},{8,0},{16,24},{24,16},{1,9},{9,1},{17,25},{25,17},{2,10},{10... | collective-permute-start | bytes 1179656 | tf_op jit(solution)/shard_map/ppermute | solution.py:711
  28.2 6.2 %collective-permute-start.8 = (bf16[16,2048]{1,0:T(8,128)(2,1)S(1)}, bf16[16,2048]{1,0:T(8,128)(2,1)S(1)}, u32[]{:S(2)}, u32[]{:S(2)}) collective-permute-start(bf16[16,2048]{1,0:T(8,128)(2,1)S(1)} %get-tuple-element.139), channel_id=1, source_target_pairs={{0,6},{1,7},{2,4},{3,5},{4,2},{5,3},{6,0},{7,1},{8,14},{9,15},{10,... | collective-permute-start | bytes 196616 | tf_op jit(solution)/shard_map/ppermute | solution.py:711
  31.8 5.6 %collective-permute-start.9 = (bf16[16,2048]{1,0:T(8,128)(2,1)S(1)}, bf16[16,2048]{1,0:T(8,128)(2,1)S(1)}, u32[]{:S(2)}, u32[]{:S(2)}) collective-permute-start(bf16[16,2048]{1,0:T(8,128)(2,1)S(1)} %get-tuple-element.140), channel_id=1, source_target_pairs={{0,7},{1,6},{2,5},{3,4},{4,3},{5,2},{6,1},{7,0},{8,15},{9,14},{10,... | collective-permute-start | bytes 196616 | tf_op jit(solution)/shard_map/ppermute | solution.py:711
  31.8 9.3 %collective-permute-start.10 = (bf16[16,2048]{1,0:T(8,128)(2,1)S(1)}, bf16[16,2048]{1,0:T(8,128)(2,1)S(1)}, u32[]{:S(2)}, u32[]{:S(2)}) collective-permute-start(bf16[16,2048]{1,0:T(8,128)(2,1)S(1)} %get-tuple-element.141), channel_id=1, source_target_pairs={{0,4},{1,5},{2,6},{3,7},{4,0},{5,1},{6,2},{7,3},{8,12},{9,13},{10,... | collective-permute-start | bytes 196616 | tf_op jit(solution)/shard_map/ppermute | solution.py:711
  34.3 8.4 %collective-permute-start.11 = (bf16[16,2048]{1,0:T(8,128)(2,1)S(1)}, bf16[16,2048]{1,0:T(8,128)(2,1)S(1)}, u32[]{:S(2)}, u32[]{:S(2)}) collective-permute-start(bf16[16,2048]{1,0:T(8,128)(2,1)S(1)} %get-tuple-element.142), channel_id=1, source_target_pairs={{0,5},{1,4},{2,7},{3,6},{4,1},{5,0},{6,3},{7,2},{8,13},{9,12},{10,... | collective-permute-start | bytes 196616 | tf_op jit(solution)/shard_map/ppermute | solution.py:711
  37.3 6.1 %collective-permute-start.12 = (bf16[16,2048]{1,0:T(8,128)(2,1)S(1)}, bf16[16,2048]{1,0:T(8,128)(2,1)S(1)}, u32[]{:S(2)}, u32[]{:S(2)}) collective-permute-start(bf16[16,2048]{1,0:T(8,128)(2,1)S(1)} %get-tuple-element.143), channel_id=1, source_target_pairs={{0,2},{1,3},{2,0},{3,1},{4,6},{5,7},{6,4},{7,5},{8,10},{9,11},{10,... | collective-permute-start | bytes 196616 | tf_op jit(solution)/shard_map/ppermute | solution.py:711
  41.1 4.1 %collective-permute-start.13 = (bf16[16,2048]{1,0:T(8,128)(2,1)S(1)}, bf16[16,2048]{1,0:T(8,128)(2,1)S(1)}, u32[]{:S(2)}, u32[]{:S(2)}) collective-permute-start(bf16[16,2048]{1,0:T(8,128)(2,1)S(1)} %get-tuple-element.144), channel_id=1, source_target_pairs={{0,3},{1,2},{2,1},{3,0},{4,7},{5,6},{6,5},{7,4},{8,11},{9,10},{10,... | collective-permute-start | bytes 196616 | tf_op jit(solution)/shard_map/ppermute | solution.py:711
  42.7 2.5 %collective-permute-start.14 = (bf16[16,2048]{1,0:T(8,128)(2,1)S(1)}, bf16[16,2048]{1,0:T(8,128)(2,1)S(1)}, u32[]{:S(2)}, u32[]{:S(2)}) collective-permute-start(bf16[16,2048]{1,0:T(8,128)(2,1)S(1)} %get-tuple-element.145), channel_id=1, source_target_pairs={{0,1},{1,0},{2,3},{3,2},{4,5},{5,4},{6,7},{7,6},{8,9},{9,8},{10,11... | collective-permute-start | bytes 196616 | tf_op jit(solution)/shard_map/ppermute | solution.py:711
  45.2 5.2 %copy-start.2 = (bf16[1024,768]{1,0:T(8,128)(2,1)S(1)}, bf16[1024,768]{1,0:T(8,128)(2,1)}, u32[]{:S(2)}) copy-start(bf16[1024,768]{1,0:T(8,128)(2,1)} %refs_0_.5) | copy-start | bytes 4718596
  45.2 5.2 %copy-start.4 = (bf16[768,192]{0,1:T(8,128)(2,1)S(1)}, bf16[768,192]{0,1:T(8,128)(2,1)}, u32[]{:S(2)}) copy-start(bf16[768,192]{0,1:T(8,128)(2,1)} %param.18) | copy-start | bytes 884740
  45.3 5.2 %copy-start.5 = (bf16[768,192]{0,1:T(8,128)(2,1)S(1)}, bf16[768,192]{0,1:T(8,128)(2,1)}, u32[]{:S(2)}) copy-start(bf16[768,192]{0,1:T(8,128)(2,1)} %param.19) | copy-start | bytes 884740
  45.3 5.2 %copy-start.6 = (bf16[768,192]{0,1:T(8,128)(2,1)S(1)}, bf16[768,192]{0,1:T(8,128)(2,1)}, u32[]{:S(2)}) copy-start(bf16[768,192]{0,1:T(8,128)(2,1)} %param.20) | copy-start | bytes 884740
  46.9 9.1 %collective-permute-start.15 = (bf16[160,384]{1,0:T(8,128)(2,1)S(1)}, bf16[160,384]{1,0:T(8,128)(2,1)S(1)}, u32[]{:S(2)}, u32[]{:S(2)}) collective-permute-start(bf16[160,384]{1,0:T(8,128)(2,1)S(1)} %get-tuple-element.148), channel_id=1, source_target_pairs={{0,8},{8,0},{16,24},{24,16},{1,9},{9,1},{17,25},{25,17},{2,10},{10... | collective-permute-start | bytes 368648 | tf_op jit(solution)/shard_map/ppermute | solution.py:711
  48.5 7.7 %collective-permute-start.16 = (bf16[160,384]{1,0:T(8,128)(2,1)S(1)}, bf16[160,384]{1,0:T(8,128)(2,1)S(1)}, u32[]{:S(2)}, u32[]{:S(2)}) collective-permute-start(bf16[160,384]{1,0:T(8,128)(2,1)S(1)} %get-tuple-element.149), channel_id=1, source_target_pairs={{0,16},{8,24},{16,0},{24,8},{1,17},{9,25},{17,1},{25,9},{2,18},{10... | collective-permute-start | bytes 368648 | tf_op jit(solution)/shard_map/ppermute | solution.py:711
  49.0 7.2 %collective-permute-start.17 = (bf16[160,384]{1,0:T(8,128)(2,1)S(1)}, bf16[160,384]{1,0:T(8,128)(2,1)S(1)}, u32[]{:S(2)}, u32[]{:S(2)}) collective-permute-start(bf16[160,384]{1,0:T(8,128)(2,1)S(1)} %get-tuple-element.150), channel_id=1, source_target_pairs={{0,24},{8,16},{16,8},{24,0},{1,25},{9,17},{17,9},{25,1},{2,26},{10... | collective-permute-start | bytes 368648 | tf_op jit(solution)/shard_map/ppermute | solution.py:711
  56.3 12.4 %collective-permute-start.18 = (bf16[192,1024]{1,0:T(8,128)(2,1)S(1)}, bf16[192,1024]{1,0:T(8,128)(2,1)S(1)}, u32[]{:S(2)}, u32[]{:S(2)}) collective-permute-start(bf16[192,1024]{1,0:T(8,128)(2,1)S(1)} %get-tuple-element.163), channel_id=1, source_target_pairs={{0,24},{8,16},{16,8},{24,0},{1,25},{9,17},{17,9},{25,1},{2,26},{10... | collective-permute-start | bytes 1179656 | tf_op jit(solution)/shard_map/ppermute | solution.py:711
  57.6 6.2 %collective-permute-start.19 = (bf16[20,384]{1,0:T(8,128)(2,1)S(1)}, bf16[20,384]{1,0:T(8,128)(2,1)S(1)}, u32[]{:S(2)}, u32[]{:S(2)}) collective-permute-start(bf16[20,384]{1,0:T(8,128)(2,1)S(1)} %get-tuple-element.168), channel_id=1, source_target_pairs={{0,6},{1,7},{2,4},{3,5},{4,2},{5,3},{6,0},{7,1},{8,14},{9,15},{10,... | collective-permute-start | bytes 46088 | tf_op jit(solution)/shard_map/ppermute | solution.py:711
  60.4 5.1 %collective-permute-start.20 = (bf16[20,384]{1,0:T(8,128)(2,1)S(1)}, bf16[20,384]{1,0:T(8,128)(2,1)S(1)}, u32[]{:S(2)}, u32[]{:S(2)}) collective-permute-start(bf16[20,384]{1,0:T(8,128)(2,1)S(1)} %get-tuple-element.169), channel_id=1, source_target_pairs={{0,7},{1,6},{2,5},{3,4},{4,3},{5,2},{6,1},{7,0},{8,15},{9,14},{10,... | collective-permute-start | bytes 46088 | tf_op jit(solution)/shard_map/ppermute | solution.py:711
  60.4 5.1 %collective-permute-start.21 = (bf16[20,384]{1,0:T(8,128)(2,1)S(1)}, bf16[20,384]{1,0:T(8,128)(2,1)S(1)}, u32[]{:S(2)}, u32[]{:S(2)}) collective-permute-start(bf16[20,384]{1,0:T(8,128)(2,1)S(1)} %get-tuple-element.170), channel_id=1, source_target_pairs={{0,4},{1,5},{2,6},{3,7},{4,0},{5,1},{6,2},{7,3},{8,12},{9,13},{10,... | collective-permute-start | bytes 46088 | tf_op jit(solution)/shard_map/ppermute | solution.py:711
  60.4 8.1 %collective-permute-start.22 = (bf16[20,384]{1,0:T(8,128)(2,1)S(1)}, bf16[20,384]{1,0:T(8,128)(2,1)S(1)}, u32[]{:S(2)}, u32[]{:S(2)}) collective-permute-start(bf16[20,384]{1,0:T(8,128)(2,1)S(1)} %get-tuple-element.171), channel_id=1, source_target_pairs={{0,5},{1,4},{2,7},{3,6},{4,1},{5,0},{6,3},{7,2},{8,13},{9,12},{10,... | collective-permute-start | bytes 46088 | tf_op jit(solution)/shard_map/ppermute | solution.py:711
  63.8 4.7 %collective-permute-start.23 = (bf16[20,384]{1,0:T(8,128)(2,1)S(1)}, bf16[20,384]{1,0:T(8,128)(2,1)S(1)}, u32[]{:S(2)}, u32[]{:S(2)}) collective-permute-start(bf16[20,384]{1,0:T(8,128)(2,1)S(1)} %get-tuple-element.172), channel_id=1, source_target_pairs={{0,2},{1,3},{2,0},{3,1},{4,6},{5,7},{6,4},{7,5},{8,10},{9,11},{10,... | collective-permute-start | bytes 46088 | tf_op jit(solution)/shard_map/ppermute | solution.py:711
  65.5 3.2 %collective-permute-start.24 = (bf16[20,384]{1,0:T(8,128)(2,1)S(1)}, bf16[20,384]{1,0:T(8,128)(2,1)S(1)}, u32[]{:S(2)}, u32[]{:S(2)}) collective-permute-start(bf16[20,384]{1,0:T(8,128)(2,1)S(1)} %get-tuple-element.173), channel_id=1, source_target_pairs={{0,3},{1,2},{2,1},{3,0},{4,7},{5,6},{6,5},{7,4},{8,11},{9,10},{10,... | collective-permute-start | bytes 46088 | tf_op jit(solution)/shard_map/ppermute | solution.py:711
  65.5 3.2 %collective-permute-start.25 = (bf16[20,384]{1,0:T(8,128)(2,1)S(1)}, bf16[20,384]{1,0:T(8,128)(2,1)S(1)}, u32[]{:S(2)}, u32[]{:S(2)}) collective-permute-start(bf16[20,384]{1,0:T(8,128)(2,1)S(1)} %get-tuple-element.174), channel_id=1, source_target_pairs={{0,1},{1,0},{2,3},{3,2},{4,5},{5,4},{6,7},{7,6},{8,9},{9,8},{10,11... | collective-permute-start | bytes 46088 | tf_op jit(solution)/shard_map/ppermute | solution.py:711
  68.7 7.1 %collective-permute-start.28 = (bf16[160,384]{1,0:T(8,128)(2,1)S(1)}, bf16[160,384]{1,0:T(8,128)(2,1)S(1)}, u32[]{:S(2)}, u32[]{:S(2)}) collective-permute-start(bf16[160,384]{1,0:T(8,128)(2,1)S(1)} %get-tuple-element.178.refs_0_), channel_id=1, source_target_pairs={{0,24},{8,16},{16,8},{24,0},{1,25},{9,17},{17,9},{25,1},{2,26},{10... | collective-permute-start | bytes 368648 | tf_op jit(solution)/shard_map/ppermute | solution.py:711
  70.3 7.1 %collective-permute-start.27 = (bf16[160,384]{1,0:T(8,128)(2,1)S(1)}, bf16[160,384]{1,0:T(8,128)(2,1)S(1)}, u32[]{:S(2)}, u32[]{:S(2)}) collective-permute-start(bf16[160,384]{1,0:T(8,128)(2,1)S(1)} %get-tuple-element.178.refs_0_), channel_id=1, source_target_pairs={{0,16},{8,24},{16,0},{24,8},{1,17},{9,25},{17,1},{25,9},{2,18},{10... | collective-permute-start | bytes 368648 | tf_op jit(solution)/shard_map/ppermute | solution.py:711
  70.8 6.7 %collective-permute-start.26 = (bf16[160,384]{1,0:T(8,128)(2,1)S(1)}, bf16[160,384]{1,0:T(8,128)(2,1)S(1)}, u32[]{:S(2)}, u32[]{:S(2)}) collective-permute-start(bf16[160,384]{1,0:T(8,128)(2,1)S(1)} %get-tuple-element.178.refs_0_), channel_id=1, source_target_pairs={{0,8},{8,0},{16,24},{24,16},{1,9},{9,1},{17,25},{25,17},{2,10},{10... | collective-permute-start | bytes 368648 | tf_op jit(solution)/shard_map/ppermute | solution.py:711
  74.8 5.2 %copy-start.10 = (f32[768]{0:T(1024)S(1)}, f32[768]{0:T(1024)}, u32[]{:S(2)}) copy-start(f32[768]{0:T(1024)} %refs_11_.3) | copy-start | bytes 9220
  84.1 3.9 %copy-start.11 = (s32[2047]{0:T(1024)S(1)}, s32[2047]{0:T(1024)}, u32[]{:S(2)}) copy-start(s32[2047]{0:T(1024)} %param.29) | copy-start | bytes 24568
  84.1 2.3 %collective-permute-start.29 = (bf16[384,768]{1,0:T(8,128)(2,1)S(1)}, bf16[384,768]{1,0:T(8,128)(2,1)S(1)}, u32[]{:S(2)}, u32[]{:S(2)}) collective-permute-start(bf16[384,768]{1,0:T(8,128)(2,1)S(1)} %get-tuple-element.204), channel_id=1, source_target_pairs={{0,1},{1,0},{2,3},{3,2},{4,5},{5,4},{6,7},{7,6},{8,9},{9,8},{10,11... | collective-permute-start | bytes 1769480 | tf_op jit(solution)/shard_map/ppermute | solution.py:711
  84.1 12.1 %collective-permute-start.31 = (bf16[272,768]{1,0:T(8,128)(2,1)S(1)}, bf16[272,768]{1,0:T(8,128)(2,1)S(1)}, u32[]{:S(2)}, u32[]{:S(2)}) collective-permute-start(bf16[272,768]{1,0:T(8,128)(2,1)S(1)} %get-tuple-element.208), channel_id=1, source_target_pairs={{0,8},{8,0},{16,24},{24,16},{1,9},{9,1},{17,25},{25,17},{2,10},{10... | collective-permute-start | bytes 1253384 | tf_op jit(solution)/shard_map/ppermute | solution.py:711
  84.9 11.2 %collective-permute-start.32 = (bf16[256,768]{1,0:T(8,128)(2,1)S(1)}, bf16[256,768]{1,0:T(8,128)(2,1)S(1)}, u32[]{:S(2)}, u32[]{:S(2)}) collective-permute-start(bf16[256,768]{1,0:T(8,128)(2,1)S(1)} %get-tuple-element.210), channel_id=1, source_target_pairs={{0,16},{8,24},{16,0},{24,8},{1,17},{9,25},{17,1},{25,9},{2,18},{10... | collective-permute-start | bytes 1179656 | tf_op jit(solution)/shard_map/ppermute | solution.py:711
  86.5 9.7 %collective-permute-start.30 = (bf16[192,768]{1,0:T(8,128)(2,1)S(1)}, bf16[192,768]{1,0:T(8,128)(2,1)S(1)}, u32[]{:S(2)}, u32[]{:S(2)}) collective-permute-start(bf16[192,768]{1,0:T(8,128)(2,1)S(1)} %get-tuple-element.206), channel_id=1, source_target_pairs={{0,2},{1,3},{2,0},{3,1},{4,6},{5,7},{6,4},{7,5},{8,10},{9,11},{10,... | collective-permute-start | bytes 884744 | tf_op jit(solution)/shard_map/ppermute | solution.py:711
  96.5 11.1 %collective-permute-start.34 = (bf16[144,768]{1,0:T(8,128)(2,1)S(1)}, bf16[144,768]{1,0:T(8,128)(2,1)S(1)}, u32[]{:S(2)}, u32[]{:S(2)}) collective-permute-start(bf16[144,768]{1,0:T(8,128)(2,1)S(1)} %get-tuple-element.224.refs_5_), channel_id=1, source_target_pairs={{0,16},{8,24},{16,0},{24,8},{1,17},{9,25},{17,1},{25,9},{2,18},{10... | collective-permute-start | bytes 663560 | tf_op jit(solution)/shard_map/ppermute | solution.py:711
  97.9 9.7 %collective-permute-start.33 = (bf16[128,768]{1,0:T(8,128)(2,1)S(1)}, bf16[128,768]{1,0:T(8,128)(2,1)S(1)}, u32[]{:S(2)}, u32[]{:S(2)}) collective-permute-start(bf16[128,768]{1,0:T(8,128)(2,1)S(1)} %get-tuple-element.223), channel_id=1, source_target_pairs={{0,8},{8,0},{16,24},{24,16},{1,9},{9,1},{17,25},{25,17},{2,10},{10... | collective-permute-start | bytes 589832 | tf_op jit(solution)/shard_map/ppermute | solution.py:711
  98.7 8.9 %collective-permute-start.35 = (bf16[96,768]{1,0:T(8,128)(2,1)S(1)}, bf16[96,768]{1,0:T(8,128)(2,1)S(1)}, u32[]{:S(2)}, u32[]{:S(2)}) collective-permute-start(bf16[96,768]{1,0:T(8,128)(2,1)S(1)} %get-tuple-element.231), channel_id=1, source_target_pairs={{0,4},{1,5},{2,6},{3,7},{4,0},{5,1},{6,2},{7,3},{8,12},{9,13},{10,... | collective-permute-start | bytes 442376 | tf_op jit(solution)/shard_map/ppermute | solution.py:711
  108.3 11.2 %collective-permute-start.38 = (bf16[256,768]{1,0:T(8,128)(2,1)S(1)}, bf16[256,768]{1,0:T(8,128)(2,1)S(1)}, u32[]{:S(2)}, u32[]{:S(2)}) collective-permute-start(bf16[256,768]{1,0:T(8,128)(2,1)S(1)} %get-tuple-element.236.own), channel_id=1, source_target_pairs={{0,16},{8,24},{16,0},{24,8},{1,17},{9,25},{17,1},{25,9},{2,18},{10... | collective-permute-start | bytes 1179656 | tf_op jit(solution)/shard_map/ppermute | solution.py:711
  109.1 10.3 %collective-permute-start.37 = (bf16[256,768]{1,0:T(8,128)(2,1)S(1)}, bf16[256,768]{1,0:T(8,128)(2,1)S(1)}, u32[]{:S(2)}, u32[]{:S(2)}) collective-permute-start(bf16[256,768]{1,0:T(8,128)(2,1)S(1)} %get-tuple-element.236.own), channel_id=1, source_target_pairs={{0,8},{8,0},{16,24},{24,16},{1,9},{9,1},{17,25},{25,17},{2,10},{10... | collective-permute-start | bytes 1179656 | tf_op jit(solution)/shard_map/ppermute | solution.py:711
  110.3 9.2 %collective-permute-start.36 = (bf16[112,768]{1,0:T(8,128)(2,1)S(1)}, bf16[112,768]{1,0:T(8,128)(2,1)S(1)}, u32[]{:S(2)}, u32[]{:S(2)}) collective-permute-start(bf16[112,768]{1,0:T(8,128)(2,1)S(1)} %get-tuple-element.235.refs_0_), channel_id=1, source_target_pairs={{0,4},{1,5},{2,6},{3,7},{4,0},{5,1},{6,2},{7,3},{8,12},{9,13},{10,... | collective-permute-start | bytes 516104 | tf_op jit(solution)/shard_map/ppermute | solution.py:711
  120.1 8.5 %collective-permute-start.41 = (bf16[208,768]{1,0:T(8,128)(2,1)S(1)}, bf16[208,768]{1,0:T(8,128)(2,1)S(1)}, u32[]{:S(2)}, u32[]{:S(2)}) collective-permute-start(bf16[208,768]{1,0:T(8,128)(2,1)S(1)} %get-tuple-element.241.refs_0_), channel_id=1, source_target_pairs={{0,2},{1,3},{2,0},{3,1},{4,6},{5,7},{6,4},{7,5},{8,10},{9,11},{10,... | collective-permute-start | bytes 958472 | tf_op jit(solution)/shard_map/ppermute | solution.py:711
  120.1 5.8 %collective-permute-start.39 = (bf16[128,768]{1,0:T(8,128)(2,1)S(1)}, bf16[128,768]{1,0:T(8,128)(2,1)S(1)}, u32[]{:S(2)}, u32[]{:S(2)}) collective-permute-start(bf16[128,768]{1,0:T(8,128)(2,1)S(1)} %get-tuple-element.238), channel_id=1, source_target_pairs={{0,8},{8,0},{16,24},{24,16},{1,9},{9,1},{17,25},{25,17},{2,10},{10... | collective-permute-start | bytes 589832 | tf_op jit(solution)/shard_map/ppermute | solution.py:711
  121.3 5.8 %collective-permute-start.40 = (bf16[128,768]{1,0:T(8,128)(2,1)S(1)}, bf16[128,768]{1,0:T(8,128)(2,1)S(1)}, u32[]{:S(2)}, u32[]{:S(2)}) collective-permute-start(bf16[128,768]{1,0:T(8,128)(2,1)S(1)} %get-tuple-element.239), channel_id=1, source_target_pairs={{0,16},{8,24},{16,0},{24,8},{1,17},{9,25},{17,1},{25,9},{2,18},{10... | collective-permute-start | bytes 589832 | tf_op jit(solution)/shard_map/ppermute | solution.py:711
  129.2 2.0 %collective-permute-start.42 = (bf16[400,768]{1,0:T(8,128)(2,1)S(1)}, bf16[400,768]{1,0:T(8,128)(2,1)S(1)}, u32[]{:S(2)}, u32[]{:S(2)}) collective-permute-start(bf16[400,768]{1,0:T(8,128)(2,1)S(1)} %get-tuple-element.243.refs_0_), channel_id=1, source_target_pairs={{0,1},{1,0},{2,3},{3,2},{4,5},{5,4},{6,7},{7,6},{8,9},{9,8},{10,11... | collective-permute-start | bytes 1843208 | tf_op jit(solution)/shard_map/ppermute | solution.py:711
where the time goes:
time: 133 us
  Pallas kernels  52.3 us (39%)
  starting transfers between devices  44.1 us (33%)
  waiting for transfers between devices  33.9 us (25%)
  local copies, waits for them, and re-layouts  1.49 us (1%)
    ppermute x43, starting transfers between devices, swap(): return lax.ppermute(x, axis, [(i, i ^ d) for i in range(size)])  44.1 us
    pallas_call x22, Pallas kernels, call(): pl.pallas_call(body, out_shape=outs, in_specs=[spec(pltpu.VMEM)] * len(ar...  38.5 us
    ppermute x43, waiting for transfers between devices, swap(): return lax.ppermute(x, axis, [(i, i ^ d) for i in range(size)])  33.9 us
    pallas_call x1, Pallas kernels, on_device(): pl.pallas_call(attend_kernel, out_shape=(shape_of(tokens, width, bf16), j...  11.3 us
  transfers between devices with their start and end apart: 43, of which 23 were waited for; matrix products, arithmetic and copies ran while one was open for 0% of the time, Pallas kernels for 29%

commit v1 on v0

--- a/solution.py
+++ b/solution.py
@@ -283,7 +283,7 @@
 
 
 def far_first(count):
-    return sorted(range(count), key=lambda d: (-(d // 2), -d if d < 2 else d))
+    return list(range(count - 2, 1, -2)) + list(range(count - 1, 2, -2)) + [1, 0]
 
 
 def by_partner(refs):

time: 133 us -> 133 us (level)
  starting transfers between devices: 44.1 us -> 41.1 us
  waiting for transfers between devices: 33.9 us -> 36.6 us
    ppermute x43, starting transfers between devices: 44.1 us -> 41.1 us  [swap(): return lax.ppermute(x, axis, [(i, i ^ d) for i in range(size)])]
    ppermute x43, waiting for transfers between devices: 33.9 us -> 36.6 us  [swap(): return lax.ppermute(x, axis, [(i, i ^ d) for i in range(size)])]
  transfers between devices with their start and end apart: 43 -> 43, of which waited for: 23 -> 21; matrix products, arithmetic and copies ran while one was open for 0% -> 0% of each run, Pallas kernels for 29% -> 29%
where the time goes in v1:
time: 133 us; the launch traced here: 132 us
  Pallas kernels  52.2 us (39%)
  starting transfers between devices  41.1 us (31%)
  waiting for transfers between devices  36.6 us (28%)
  local copies, waits for them, and re-layouts  1.49 us (1%)
    ppermute x43, starting transfers between devices, swap(): return lax.ppermute(x, axis, [(i, i ^ d) for i in range(size)])  41.1 us
    pallas_call x22, Pallas kernels, call(): pl.pallas_call(body, out_shape=outs, in_specs=[spec(pltpu.VMEM)] * len(ar...  38.5 us
    ppermute x43, waiting for transfers between devices, swap(): return lax.ppermute(x, axis, [(i, i ^ d) for i in range(size)])  36.6 us
    pallas_call x1, Pallas kernels, on_device(): pl.pallas_call(attend_kernel, out_shape=(shape_of(tokens, width, bf16), j...  11.3 us
  transfers between devices with their start and end apart: 43, of which 21 were waited for; matrix products, arithmetic and copies ran while one was open for 0% of the time, Pallas kernels for 29%

profile of v1, /device:TPU:0, one launch (start us, length us, event | category | flops | bytes accessed | tf_op | source)
XLA Modules:
  0.0 132.4 jit_solution(9711742877954900012)
XLA Ops:
  0.7 3.0 %collective-permute-start = (bf16[192,768]{1,0:T(8,128)(2,1)}, bf16[192,768]{1,0:T(8,128)(2,1)S(1)}, u32[]{:S(2)}, u32[]{:S(2)}) collective-permute-start(bf16[192,768]{1,0:T(8,128)(2,1)} %refs_10_.1), channel_id=1, source_target_pairs={{0,8},{8,0},{16,24},{24,16},{1,9},{9,1},{17,25},{25,17},{2,10},{10... | collective-permute-start | bytes 884744 | tf_op jit(solution)/shard_map/ppermute | solution.py:711
  3.7 1.5 %collective-permute-start.5 = (bf16[192,768]{1,0:T(8,128)(2,1)}, bf16[192,768]{1,0:T(8,128)(2,1)S(1)}, u32[]{:S(2)}, u32[]{:S(2)}) collective-permute-start(bf16[192,768]{1,0:T(8,128)(2,1)} %refs_10_.1), channel_id=1, source_target_pairs={{0,24},{8,16},{16,8},{24,0},{1,25},{9,17},{17,9},{25,1},{2,26},{10... | collective-permute-start | bytes 884744 | tf_op jit(solution)/shard_map/ppermute | solution.py:711
  5.2 11.3 %attend.1 = (bf16[1024,768]{1,0:T(8,128)(2,1)S(1)}, bf16[3,1024,1024]{2,1,0:T(8,128)(2,1)S(1)}, bf16[3,1024,64]{2,1,0:T(8,128)(2,1)S(1)}, bf16[192,1024]{1,0:T(8,128)(2,1)S(1)}, bf16[80,384]{1,0:T(8,128)(2,1)S(1)}) custom-call(bf16[1024,768]{1,0:T(8,128)(2,1)} %refs_5_.1, f32[768]{0:T(1024)} %refs_11_.3, bf16[192,768]{1,0:T(8,128)(2,1)} %bitcast.15, ...), custom_call_target="tpu_custom_call" | custom-call | flops 1 | bytes 1 | tf_op jit(solution)/shard_map/attend/pallas_call | solution.py:790
  16.6 3.0 %collective-permute-start.3 = (bf16[80,384]{1,0:T(8,128)(2,1)S(1)}, bf16[80,384]{1,0:T(8,128)(2,1)S(1)}, u32[]{:S(2)}, u32[]{:S(2)}) collective-permute-start(bf16[80,384]{1,0:T(8,128)(2,1)S(1)} %pass.1.refs_8_.refs_0_.refs_11_), channel_id=1, source_target_pairs={{0,24},{8,16},{16,8},{24,0},{1,25},{9,17},{17,9},{25,1},{2,26},{10... | collective-permute-start | bytes 184328 | tf_op jit(solution)/shard_map/ppermute | solution.py:711
  20.6 1.4 %copy-done.1 = bf16[1024,768]{1,0:T(8,128)(2,1)S(1)} copy-done((bf16[1024,768]{1,0:T(8,128)(2,1)S(1)}, bf16[1024,768]{1,0:T(8,128)(2,1)}, u32[]{:S(2)}) %copy-start.1) | copy-done | bytes 1572888
  22.0 1.1 place.1
  23.2 0.6 collective-permute-done.2.refs_2_
  24.3 1.7 %route.1 = (f32[192,768]{1,0:T(8,128)S(1)}, f32[192,768]{1,0:T(8,128)S(1)}, f32[192,8]{1,0:T(8,128)S(1)}, bf16[192,1024]{1,0:T(8,128)(2,1)S(1)}, bf16[16,2048]{1...) custom-call(bf16[80,384]{1,0:T(8,128)(2,1)S(1)} %pass.1.refs_8_.refs, ...), custom_call_target="tpu_custom_call" | custom-call | flops 1 | bytes 1 | tf_op jit(solution)/shard_map/route/pallas_call | solution.py:74
  26.0 1.6 %collective-permute-start.7 = (bf16[192,1024]{1,0:T(8,128)(2,1)S(1)}, bf16[192,1024]{1,0:T(8,128)(2,1)S(1)}, u32[]{:S(2)}, u32[]{:S(2)}) collective-permute-start(bf16[192,1024]{1,0:T(8,128)(2,1)S(1)} %get-tuple-element.138), channel_id=1, source_target_pairs={{0,16},{8,24},{16,0},{24,8},{1,17},{9,25},{17,1},{25,9},{2,18},{10... | collective-permute-start | bytes 1179656 | tf_op jit(solution)/shard_map/ppermute | solution.py:711
  27.6 0.5 collective-permute-start.6
  28.2 3.6 %collective-permute-start.8 = (bf16[16,2048]{1,0:T(8,128)(2,1)S(1)}, bf16[16,2048]{1,0:T(8,128)(2,1)S(1)}, u32[]{:S(2)}, u32[]{:S(2)}) collective-permute-start(bf16[16,2048]{1,0:T(8,128)(2,1)S(1)} %get-tuple-element.139), channel_id=1, source_target_pairs={{0,6},{1,7},{2,4},{3,5},{4,2},{5,3},{6,0},{7,1},{8,14},{9,15},{10,... | collective-permute-start | bytes 196616 | tf_op jit(solution)/shard_map/ppermute | solution.py:711
  31.8 0.8 collective-permute-start.10
  32.5 2.2 %collective-permute-done.8.refs_0_ = bf16[16,2048]{1,0:T(8,128)(2,1)S(1)} collective-permute-done((bf16[16,2048]{1,0:T(8,128)(2,1)S(1)}, bf16[16,2048]{1,0:T(8,128)(2,1)S(1)}, u32[]{:S(2)}, u32[]{:S(2)}) %collective-permute-start.8) | collective-permute-done | bytes 65568 | tf_op jit(solution)/shard_map/ppermute | solution.py:711
  34.8 2.2 %collective-permute-done.9.refs_1_ = bf16[16,2048]{1,0:T(8,128)(2,1)S(1)} collective-permute-done((bf16[16,2048]{1,0:T(8,128)(2,1)S(1)}, bf16[16,2048]{1,0:T(8,128)(2,1)S(1)}, u32[]{:S(2)}, u32[]{:S(2)}) %collective-permute-start.9) | collective-permute-done | bytes 65568 | tf_op jit(solution)/shard_map/ppermute | solution.py:711
  36.9 1.2 collective-permute-start.13
  38.2 2.8 %collective-permute-done.11.refs_3_ = bf16[16,2048]{1,0:T(8,128)(2,1)S(1)} collective-permute-done((bf16[16,2048]{1,0:T(8,128)(2,1)S(1)}, bf16[16,2048]{1,0:T(8,128)(2,1)S(1)}, u32[]{:S(2)}, u32[]{:S(2)}) %collective-permute-start.11) | collective-permute-done | bytes 65568 | tf_op jit(solution)/shard_map/ppermute | solution.py:711
  41.0 2.6 %collective-permute-done.12.refs_4_ = bf16[16,2048]{1,0:T(8,128)(2,1)S(1)} collective-permute-done((bf16[16,2048]{1,0:T(8,128)(2,1)S(1)}, bf16[16,2048]{1,0:T(8,128)(2,1)S(1)}, u32[]{:S(2)}, u32[]{:S(2)}) %collective-permute-start.12) | collective-permute-done | bytes 65568 | tf_op jit(solution)/shard_map/ppermute | solution.py:711
  43.6 1.6 %expert.1 = (bf16[160,384]{1,0:T(8,128)(2,1)S(1)}, bf16[160,384]{1,0:T(8,128)(2,1)S(1)}, bf16[160,384]{1,0:T(8,128)(2,1)S(1)}, bf16[160,384]{1,0:T(8,128)(2,1)S(...) custom-call(bf16[16,2048]{1,0:T(8,128)(2,1)S(1)} %collective-permute, ...), custom_call_target="tpu_custom_call" | custom-call | flops 1 | bytes 1 | tf_op jit(solution)/shard_map/expert/pallas_call | solution.py:74
  45.2 1.6 %collective-permute-start.15 = (bf16[160,384]{1,0:T(8,128)(2,1)S(1)}, bf16[160,384]{1,0:T(8,128)(2,1)S(1)}, u32[]{:S(2)}, u32[]{:S(2)}) collective-permute-start(bf16[160,384]{1,0:T(8,128)(2,1)S(1)} %get-tuple-element.148), channel_id=1, source_target_pairs={{0,8},{8,0},{16,24},{24,16},{1,9},{9,1},{17,25},{25,17},{2,10},{10... | collective-permute-start | bytes 368648 | tf_op jit(solution)/shard_map/ppermute | solution.py:711
  47.3 1.5 %collective-permute-start.17 = (bf16[160,384]{1,0:T(8,128)(2,1)S(1)}, bf16[160,384]{1,0:T(8,128)(2,1)S(1)}, u32[]{:S(2)}, u32[]{:S(2)}) collective-permute-start(bf16[160,384]{1,0:T(8,128)(2,1)S(1)} %get-tuple-element.150), channel_id=1, source_target_pairs={{0,24},{8,16},{16,8},{24,0},{1,25},{9,17},{17,9},{25,1},{2,26},{10... | collective-permute-start | bytes 368648 | tf_op jit(solution)/shard_map/ppermute | solution.py:711
  48.8 2.9 %prep.1 = (bf16[3,1024,64]{2,1,0:T(8,128)(2,1)S(1)}, bf16[3,256,1024]{2,1,0:T(8,128)(2,1)S(1)}, bf16[3,1024,64]{2,1,0:T(8,128)(2,1)S(1)}, bf16[192,1024]{1,0:T(8...) custom-call(bf16[1024,768]{1,0:T(8,128)(2,1)S(1)} %copy-done.2, ...), custom_call_target="tpu_custom_call" | custom-call | flops 1 | bytes 8388608 | tf_op jit(solution)/shard_map/prep/pallas_call | solution.py:74
  51.7 2.5 %masked_back.3 = (f32[1024,64]{1,0:T(8,128)S(1)}, f32[64,1024]{1,0:T(8,128)S(1)}, f32[64,1024]{1,0:T(8,128)S(1)}, f32[8,2048]{1,0:T(8,128)S(1)}, bf16[192,1024]{1,0:T(8,128)(2,1)S(1)}, /*index=5*/f32[8,128]{1,0:T(8,128)S(1)}) custom-call(bf16[3,1024,64]{2,1,0:T(8,128)(2,1)S(1)} %get-tuple-element.154.refs_0_, ...), custom_call_target="tpu_custom_call" | custom-call | flops 1 | bytes 11534336 | tf_op jit(solution)/shard_map/masked_back/pallas_call | solution.py:74
  54.6 1.4 %collective-permute-start.18 = (bf16[192,1024]{1,0:T(8,128)(2,1)S(1)}, bf16[192,1024]{1,0:T(8,128)(2,1)S(1)}, u32[]{:S(2)}, u32[]{:S(2)}) collective-permute-start(bf16[192,1024]{1,0:T(8,128)(2,1)S(1)} %get-tuple-element.163), channel_id=1, source_target_pairs={{0,24},{8,16},{16,8},{24,0},{1,25},{9,17},{17,9},{25,1},{2,26},{10... | collective-permute-start | bytes 1179656 | tf_op jit(solution)/shard_map/ppermute | solution.py:711
  56.0 1.9 %collective-permute-start.19 = (bf16[20,384]{1,0:T(8,128)(2,1)S(1)}, bf16[20,384]{1,0:T(8,128)(2,1)S(1)}, u32[]{:S(2)}, u32[]{:S(2)}) collective-permute-start(bf16[20,384]{1,0:T(8,128)(2,1)S(1)} %get-tuple-element.168), channel_id=1, source_target_pairs={{0,6},{1,7},{2,4},{3,5},{4,2},{5,3},{6,0},{7,1},{8,14},{9,15},{10,... | collective-permute-start | bytes 46088 | tf_op jit(solution)/shard_map/ppermute | solution.py:711
  58.3 2.1 %collective-permute-start.21 = (bf16[20,384]{1,0:T(8,128)(2,1)S(1)}, bf16[20,384]{1,0:T(8,128)(2,1)S(1)}, u32[]{:S(2)}, u32[]{:S(2)}) collective-permute-start(bf16[20,384]{1,0:T(8,128)(2,1)S(1)} %get-tuple-element.170), channel_id=1, source_target_pairs={{0,2},{1,3},{2,0},{3,1},{4,6},{5,7},{6,4},{7,5},{8,10},{9,11},{10,... | collective-permute-start | bytes 46088 | tf_op jit(solution)/shard_map/ppermute | solution.py:711
  60.4 1.3 collective-permute-done.19.refs_0_
  61.7 0.8 collective-permute-done.20.refs_1_
  62.5 1.4 %collective-permute-start.24 = (bf16[20,384]{1,0:T(8,128)(2,1)S(1)}, bf16[20,384]{1,0:T(8,128)(2,1)S(1)}, u32[]{:S(2)}, u32[]{:S(2)}) collective-permute-start(bf16[20,384]{1,0:T(8,128)(2,1)S(1)} %get-tuple-element.173), channel_id=1, source_target_pairs={{0,3},{1,2},{2,1},{3,0},{4,7},{5,6},{6,5},{7,4},{8,11},{9,10},{10,... | collective-permute-start | bytes 46088 | tf_op jit(solution)/shard_map/ppermute | solution.py:711
  63.9 0.7 collective-permute-start.25
  64.6 2.5 %masked_back.4 = (f32[1024,64]{1,0:T(8,128)S(1)}, f32[64,1024]{1,0:T(8,128)S(1)}, f32[64,1024]{1,0:T(8,128)S(1)}, f32[8,2048]{1,0:T(8,128)S(1)}, bf16[192,1024]{1,0:T(8,128)(2,1)S(1)}, /*index=5*/f32[8,128]{1,0:T(8,128)S(1)}) custom-call(bf16[3,1024,64]{2,1,0:T(8,128)(2,1)S(1)} %get-tuple-element.154.refs_0_, ...), custom_call_target="tpu_custom_call" | custom-call | flops 1 | bytes 11534336 | tf_op jit(solution)/shard_map/masked_back/pallas_call | solution.py:74
  67.2 1.7 %collective-permute-start.28 = (bf16[160,384]{1,0:T(8,128)(2,1)S(1)}, bf16[160,384]{1,0:T(8,128)(2,1)S(1)}, u32[]{:S(2)}, u32[]{:S(2)}) collective-permute-start(bf16[160,384]{1,0:T(8,128)(2,1)S(1)} %get-tuple-element.178.refs_0_), channel_id=1, source_target_pairs={{0,24},{8,16},{16,8},{24,0},{1,25},{9,17},{17,9},{25,1},{2,26},{10... | collective-permute-start | bytes 368648 | tf_op jit(solution)/shard_map/ppermute | solution.py:711
  68.9 0.5 collective-permute-start.27
  69.5 1.3 %collective-permute-start.26 = (bf16[160,384]{1,0:T(8,128)(2,1)S(1)}, bf16[160,384]{1,0:T(8,128)(2,1)S(1)}, u32[]{:S(2)}, u32[]{:S(2)}) collective-permute-start(bf16[160,384]{1,0:T(8,128)(2,1)S(1)} %get-tuple-element.178.refs_0_), channel_id=1, source_target_pairs={{0,8},{8,0},{16,24},{24,16},{1,9},{9,1},{17,25},{25,17},{2,10},{10... | collective-permute-start | bytes 368648 | tf_op jit(solution)/shard_map/ppermute | solution.py:711
  70.8 2.5 %masked_back.5 = (f32[1024,64]{1,0:T(8,128)S(1)}, f32[64,1024]{1,0:T(8,128)S(1)}, f32[64,1024]{1,0:T(8,128)S(1)}, f32[8,2048]{1,0:T(8,128)S(1)}, bf16[192,1024]{1,0:T(8,128)(2,1)S(1)}, /*index=5*/f32[8,128]{1,0:T(8,128)S(1)}) custom-call(bf16[3,1024,64]{2,1,0:T(8,128)(2,1)S(1)} %get-tuple-element.154.refs_0_, ...), custom_call_target="tpu_custom_call" | custom-call | flops 1 | bytes 11534336 | tf_op jit(solution)/shard_map/masked_back/pallas_call | solution.py:74
  73.3 1.0 collective-permute-done.28.refs_3_
  74.4 1.7 %collective-permute-done.27.refs_2_ = bf16[160,384]{1,0:T(8,128)(2,1)S(1)} collective-permute-done((bf16[160,384]{1,0:T(8,128)(2,1)S(1)}, bf16[160,384]{1,0:T(8,128)(2,1)S(1)}, u32[]{:S(2)}, u32[]{:S(2)}) %collective-permute-start.27) | collective-permute-done | bytes 122912 | tf_op jit(solution)/shard_map/ppermute | solution.py:711
  76.1 2.4 %slot_back.1 = (f32[192,768]{1,0:T(8,128)S(1)}, f32[192,768]{1,0:T(8,128)S(1)}, f32[16,768]{1,0:T(8,128)S(1)}, f32[192,768]{1,0:T(8,128)S(1)}, bf16[3,192,64]{2,...) custom-call(bf16[160,384]{1,0:T(8,128)(2,1)S(1)} %get-tuple-element.178.refs_0_, ...), custom_call_target="tpu_custom_call" | custom-call | flops 1 | bytes 1 | tf_op jit(solution)/shard_map/slot_back/pallas_call | solution.py:74
  78.6 4.1 %sparse_back.1 = (bf16[256,768]{1,0:T(8,128)(2,1)S(1)}, bf16[272,768]{1,0:T(8,128)(2,1)S(1)}, bf16[256,768]{1,0:T(8,128)(2,1)S(1)}, bf16[128,768]{1,0:T(8,128)(2...) custom-call(bf16[3,192,64]{2,1,0:T(8,128)(2,1)S(1)} %get-tuple-eleme, ...), custom_call_target="tpu_custom_call" | custom-call | flops 1 | bytes 1 | tf_op jit(solution)/shard_map/sparse_back/pallas_call | solution.py:74
  82.7 0.7 collective-permute-start.31
  83.5 1.5 %collective-permute-start.32 = (bf16[256,768]{1,0:T(8,128)(2,1)S(1)}, bf16[256,768]{1,0:T(8,128)(2,1)S(1)}, u32[]{:S(2)}, u32[]{:S(2)}) collective-permute-start(bf16[256,768]{1,0:T(8,128)(2,1)S(1)} %get-tuple-element.210), channel_id=1, source_target_pairs={{0,16},{8,24},{16,0},{24,8},{1,17},{9,25},{17,1},{25,9},{2,18},{10... | collective-permute-start | bytes 1179656 | tf_op jit(solution)/shard_map/ppermute | solution.py:711
  85.1 0.5 collective-permute-start.30
  85.6 4.7 %bias_grad.1 = (f32[16,768]{1,0:T(8,128)S(1)}, f32[8,128]{1,0:T(8,128)S(1)}) custom-call(bf16[3,192,1024]{2,1,0:T(8,128)(2,1)S(1)} %get-tuple-element.212.refs_0_, bf16[1024,192]{1,0:T(8,128)(2,1)S(1)} %get-tuple-element.152.refs_6_.refs_1_, s32[1,2047]{1,0:T(1,128)S(1)} %bitcast.29, f32[16,768]{1,0:T(8,128)S(1)} %get-tuple-element.211.refs_3_.refs_6_, ...), custom_call_target="tpu_custom_call" | custom-call | flops 1 | bytes 16777216 | tf_op jit(solution)/shard_map/bias_grad/pallas_call | solution.py:74
  90.3 4.4 %collective-permute-done.32.refs_5_.refs_2_ = bf16[256,768]{1,0:T(8,128)(2,1)S(1)} collective-permute-done((bf16[256,768]{1,0:T(8,128)(2,1)S(1)}, bf16[256,768]{1,0:T(8,128)(2,1)S(1)}, u32[]{:S(2)}, u32[]{:S(2)}) %collective-permute-start.32) | collective-permute-done | bytes 393248 | tf_op jit(solution)/shard_map/ppermute | solution.py:711
  95.1 1.4 %collective-permute-start.34 = (bf16[144,768]{1,0:T(8,128)(2,1)S(1)}, bf16[144,768]{1,0:T(8,128)(2,1)S(1)}, u32[]{:S(2)}, u32[]{:S(2)}) collective-permute-start(bf16[144,768]{1,0:T(8,128)(2,1)S(1)} %get-tuple-element.224.refs_5_), channel_id=1, source_target_pairs={{0,16},{8,24},{16,0},{24,8},{1,17},{9,25},{17,1},{25,9},{2,18},{10... | collective-permute-start | bytes 663560 | tf_op jit(solution)/shard_map/ppermute | solution.py:711
  96.5 0.8 collective-permute-start.33
  97.3 0.9 collective-permute-start.35
  98.3 2.8 %expert_grad.1 = (f32[1,768,768]{2,1,0:T(8,128)}, f32[1,768,768]{2,1,0:T(8,128)}, f32[8,128]{1,0:T(8,128)S(1)}) custom-call(bf16[192,768]{1,0:T(8,128)(2,1)S(1)} %get-tuple-element.164.refs_0_, bf16[192,768]{1,0:T(8,128)(2,1)S(1)} %get-tuple-element.165.refs_1_, bf16[192,768]{1,0:T(8,128)(2,1)S(1)} %get-tuple-element.166.refs_2_, ...), custom_call_target="tpu_custom_call" | custom-call | flops 1 | bytes 10485760 | tf_op jit(solution)/shard_map/expert_grad/pallas_call | solution.py:74
  101.1 2.3 %hidden.1 = (f32[1024,768]{1,0:T(8,128)S(1)}, f32[8,128]{1,0:T(8,128)S(1)}) custom-call(bf16[192,1024]{1,0:T(8,128)(2,1)S(1)} %get-tuple-element.133.refs_9_.refs_7_.refs_0_, bf16[192,1024]{1,0:T(8,128)(2,1)S(1)} %collective-permute-done.6.refs_10_.refs_1_, bf16[192,1024]{1,0:T(8,128)(2,1)S(1)} %collective-permute-done.7.refs_11_.refs_2_, ...), custom_call_target="tpu_custom_call" | custom-call | flops 1 | bytes 6291456 | tf_op jit(solution)/shard_map/hidden/pallas_call | solution.py:74
  103.4 2.7 %collective-permute-done.35.refs_13_ = bf16[96,768]{1,0:T(8,128)(2,1)S(1)} collective-permute-done((bf16[96,768]{1,0:T(8,128)(2,1)S(1)}, bf16[96,768]{1,0:T(8,128)(2,1)S(1)}, u32[]{:S(2)}, u32[]{:S(2)}) %collective-permute-start.35) | collective-permute-done | bytes 147488 | tf_op jit(solution)/shard_map/ppermute | solution.py:711
  106.1 0.7 first_norm.1
  106.8 1.0 collective-permute-start.38
  107.7 1.1 collective-permute-start.37
  108.9 3.2 %output.1 = (f32[1024,768]{1,0:T(8,128)}, f32[8,128]{1,0:T(8,128)S(1)}) custom-call(f32[1024,768]{1,0:T(8,128)S(1)} %get-tuple-element.220.refs_0_, bf16[1024,192]{1,0:T(8,128)(2,1)S(1)} %get-tuple-element.152.refs_6_.refs_1_, f32[192,768]{1,0:T(8,128)S(1)} %get-tuple-element.221.refs_2_, f32[8,128]{1,0:T(8,128)S(1)} %get-tuple-element.233.refs_3_), custom_call_target="tpu_custom_call" | custom-call | flops 1 | bytes 10485760 | tf_op jit(solution)/shard_map/output/pallas_call | solution.py:74
  112.1 6.0 %collective-permute-done.36.refs_1_ = bf16[112,768]{1,0:T(8,128)(2,1)S(1)} collective-permute-done((bf16[112,768]{1,0:T(8,128)(2,1)S(1)}, bf16[112,768]{1,0:T(8,128)(2,1)S(1)}, u32[]{:S(2)}, u32[]{:S(2)}) %collective-permute-start.36) | collective-permute-done | bytes 172064 | tf_op jit(solution)/shard_map/ppermute | solution.py:711
  118.1 0.6 pair.2
  118.8 1.3 collective-permute-start.39
  120.1 0.9 collective-permute-start.40
  120.9 1.5 %spread_near.1 = (f32[1024,768]{1,0:T(8,128)}, f32[8,128]{1,0:T(8,128)S(1)}) custom-call(bf16[256,768]{1,0:T(8,128)(2,1)S(1)} %get-tuple-element.236.own, bf16[256,768]{1,0:T(8,128)(2,1)S(1)} %collective-permute-done.37.refs_2_.got_1, bf16[256,768]{1,0:T(8,128)(2,1)S(1)} %collective-permute-done.38.refs_3_.got_2), custom_call_target="tpu_custom_call" | custom-call | flops 1 | bytes 5242880 | tf_op jit(solution)/shard_map/spread_near/pallas_call | solution.py:1079
  122.4 3.2 %collective-permute-done.39.last_1.refs_2_ = bf16[128,768]{1,0:T(8,128)(2,1)S(1)} collective-permute-done((bf16[128,768]{1,0:T(8,128)(2,1)S(1)}, bf16[128,768]{1,0:T(8,128)(2,1)S(1)}, u32[]{:S(2)}, u32[]{:S(2)}) %collective-permute-start.39) | collective-permute-done | bytes 196640 | tf_op jit(solution)/shard_map/ppermute | solution.py:711
  125.9 2.4 %collective-permute-done.41.refs_1_ = bf16[208,768]{1,0:T(8,128)(2,1)S(1)} collective-permute-done((bf16[208,768]{1,0:T(8,128)(2,1)S(1)}, bf16[208,768]{1,0:T(8,128)(2,1)S(1)}, u32[]{:S(2)}, u32[]{:S(2)}) %collective-permute-start.41) | collective-permute-done | bytes 319520 | tf_op jit(solution)/shard_map/ppermute | solution.py:711
  128.2 0.6 pair.3
  128.9 0.9 spread_far.1
  129.8 1.1 collective-permute-done.42.refs_1_
  130.9 1.5 %weights_out.1 = (f32[192,768]{1,0:T(8,128)}, f32[192,768]{1,0:T(8,128)}, f32[192,768]{1,0:T(8,128)}, f32[192,768]{1,0:T(8,128)}, f32[768]{0:T(1024)}, /*index=5...) custom-call(bf16[400,768]{1,0:T(8,128)(2,1)S(1)} %get-tuple-element.243.refs_0_, ...), custom_call_target="tpu_custom_call" | custom-call | flops 1 | bytes 1 | tf_op jit(solution)/shard_map/weights_out/pallas_call | solution.py:74
  (77 shorter events, 4.0 us)
Async XLA Ops:
  0.6 19.9 %copy-start.3 = (bf16[192,768]{1,0:T(8,128)(2,1)S(1)}, bf16[192,768]{1,0:T(8,128)(2,1)}, u32[]{:S(2)}) copy-start(bf16[192,768]{1,0:T(8,128)(2,1)} %refs_10_.1) | copy-start | bytes 884740
  0.7 19.9 %copy-start = (bf16[1024,768]{1,0:T(8,128)(2,1)S(1)}, bf16[1024,768]{1,0:T(8,128)(2,1)}, u32[]{:S(2)}) copy-start(bf16[1024,768]{1,0:T(8,128)(2,1)} %refs_5_.1) | copy-start | bytes 4718596
  0.7 19.9 %copy-start.13 = (s32[1024]{0:T(1024)S(1)}, s32[1024]{0:T(1024)}, u32[]{:S(2)}) copy-start(s32[1024]{0:T(1024)} %param.28) | copy-start | bytes 12292
  0.7 19.9 %copy-start.12 = (s32[1024]{0:T(1024)S(1)}, s32[1024]{0:T(1024)}, u32[]{:S(2)}) copy-start(s32[1024]{0:T(1024)} %param.27) | copy-start | bytes 12292
  0.7 15.9 %collective-permute-start = (bf16[192,768]{1,0:T(8,128)(2,1)}, bf16[192,768]{1,0:T(8,128)(2,1)S(1)}, u32[]{:S(2)}, u32[]{:S(2)}) collective-permute-start(bf16[192,768]{1,0:T(8,128)(2,1)} %refs_10_.1), channel_id=1, source_target_pairs={{0,8},{8,0},{16,24},{24,16},{1,9},{9,1},{17,25},{25,17},{2,10},{10... | collective-permute-start | bytes 884744 | tf_op jit(solution)/shard_map/ppermute | solution.py:711
  3.7 16.5 %collective-permute-start.5 = (bf16[192,768]{1,0:T(8,128)(2,1)}, bf16[192,768]{1,0:T(8,128)(2,1)S(1)}, u32[]{:S(2)}, u32[]{:S(2)}) collective-permute-start(bf16[192,768]{1,0:T(8,128)(2,1)} %refs_10_.1), channel_id=1, source_target_pairs={{0,24},{8,16},{16,8},{24,0},{1,25},{9,17},{17,9},{25,1},{2,26},{10... | collective-permute-start | bytes 884744 | tf_op jit(solution)/shard_map/ppermute | solution.py:711
  5.2 15.4 %collective-permute-start.4 = (bf16[192,768]{1,0:T(8,128)(2,1)}, bf16[192,768]{1,0:T(8,128)(2,1)S(1)}, u32[]{:S(2)}, u32[]{:S(2)}) collective-permute-start(bf16[192,768]{1,0:T(8,128)(2,1)} %refs_10_.1), channel_id=1, source_target_pairs={{0,16},{8,24},{16,0},{24,8},{1,17},{9,25},{17,1},{25,9},{2,18},{10... | collective-permute-start | bytes 884744 | tf_op jit(solution)/shard_map/ppermute | solution.py:711
  16.6 7.7 %copy-start.9 = (f32[768,8]{0,1:T(8,128)S(1)}, f32[768,8]{0,1:T(8,128)}, u32[]{:S(2)}) copy-start(f32[768,8]{0,1:T(8,128)} %param.24) | copy-start | bytes 73732
  16.6 7.7 %copy-start.14 = (f32[768]{0:T(1024)S(1)}, f32[768]{0:T(1024)}, u32[]{:S(2)}) copy-start(f32[768]{0:T(1024)} %refs_9_.1) | copy-start | bytes 9220
  16.6 6.5 %collective-permute-start.3 = (bf16[80,384]{1,0:T(8,128)(2,1)S(1)}, bf16[80,384]{1,0:T(8,128)(2,1)S(1)}, u32[]{:S(2)}, u32[]{:S(2)}) collective-permute-start(bf16[80,384]{1,0:T(8,128)(2,1)S(1)} %pass.1.refs_8_.refs_0_.refs_11_), channel_id=1, source_target_pairs={{0,24},{8,16},{16,8},{24,0},{1,25},{9,17},{17,9},{25,1},{2,26},{10... | collective-permute-start | bytes 184328 | tf_op jit(solution)/shard_map/ppermute | solution.py:711
  19.6 4.2 %collective-permute-start.2 = (bf16[80,384]{1,0:T(8,128)(2,1)S(1)}, bf16[80,384]{1,0:T(8,128)(2,1)S(1)}, u32[]{:S(2)}, u32[]{:S(2)}) collective-permute-start(bf16[80,384]{1,0:T(8,128)(2,1)S(1)} %pass.1.refs_8_.refs_0_.refs_11_), channel_id=1, source_target_pairs={{0,16},{8,24},{16,0},{24,8},{1,17},{9,25},{17,1},{25,9},{2,18},{10... | collective-permute-start | bytes 184328 | tf_op jit(solution)/shard_map/ppermute | solution.py:711
  20.1 4.2 %collective-permute-start.1 = (bf16[80,384]{1,0:T(8,128)(2,1)S(1)}, bf16[80,384]{1,0:T(8,128)(2,1)S(1)}, u32[]{:S(2)}, u32[]{:S(2)}) collective-permute-start(bf16[80,384]{1,0:T(8,128)(2,1)S(1)} %pass.1.refs_8_.refs_0_.refs_11_), channel_id=1, source_target_pairs={{0,8},{8,0},{16,24},{24,16},{1,9},{9,1},{17,25},{25,17},{2,10},{10... | collective-permute-start | bytes 184328 | tf_op jit(solution)/shard_map/ppermute | solution.py:711
  20.6 1.4 %copy-start.1 = (bf16[1024,768]{1,0:T(8,128)(2,1)S(1)}, bf16[1024,768]{1,0:T(8,128)(2,1)}, u32[]{:S(2)}) copy-start(bf16[1024,768]{1,0:T(8,128)(2,1)} %refs_0_.5) | copy-start | bytes 4718596
  23.1 20.4 %copy-start.7 = (bf16[1,768,768]{2,1,0:T(8,128)(2,1)S(1)}, bf16[1,768,768]{2,1,0:T(8,128)(2,1)}, u32[]{:S(2)}) copy-start(bf16[1,768,768]{2,1,0:T(8,128)(2,1)} %param.25) | copy-start | bytes 3538948
  23.1 20.4 %copy-start.8 = (bf16[1,768,768]{2,1,0:T(8,128)(2,1)S(1)}, bf16[1,768,768]{2,1,0:T(8,128)(2,1)}, u32[]{:S(2)}) copy-start(bf16[1,768,768]{2,1,0:T(8,128)(2,1)} %param.26) | copy-start | bytes 3538948
  26.0 17.5 %collective-permute-start.7 = (bf16[192,1024]{1,0:T(8,128)(2,1)S(1)}, bf16[192,1024]{1,0:T(8,128)(2,1)S(1)}, u32[]{:S(2)}, u32[]{:S(2)}) collective-permute-start(bf16[192,1024]{1,0:T(8,128)(2,1)S(1)} %get-tuple-element.138), channel_id=1, source_target_pairs={{0,16},{8,24},{16,0},{24,8},{1,17},{9,25},{17,1},{25,9},{2,18},{10... | collective-permute-start | bytes 1179656 | tf_op jit(solution)/shard_map/ppermute | solution.py:711
  27.6 15.9 %collective-permute-start.6 = (bf16[192,1024]{1,0:T(8,128)(2,1)S(1)}, bf16[192,1024]{1,0:T(8,128)(2,1)S(1)}, u32[]{:S(2)}, u32[]{:S(2)}) collective-permute-start(bf16[192,1024]{1,0:T(8,128)(2,1)S(1)} %get-tuple-element.138), channel_id=1, source_target_pairs={{0,8},{8,0},{16,24},{24,16},{1,9},{9,1},{17,25},{25,17},{2,10},{10... | collective-permute-start | bytes 1179656 | tf_op jit(solution)/shard_map/ppermute | solution.py:711
  28.2 6.6 %collective-permute-start.8 = (bf16[16,2048]{1,0:T(8,128)(2,1)S(1)}, bf16[16,2048]{1,0:T(8,128)(2,1)S(1)}, u32[]{:S(2)}, u32[]{:S(2)}) collective-permute-start(bf16[16,2048]{1,0:T(8,128)(2,1)S(1)} %get-tuple-element.139), channel_id=1, source_target_pairs={{0,6},{1,7},{2,4},{3,5},{4,2},{5,3},{6,0},{7,1},{8,14},{9,15},{10,... | collective-permute-start | bytes 196616 | tf_op jit(solution)/shard_map/ppermute | solution.py:711
  31.8 5.2 %collective-permute-start.9 = (bf16[16,2048]{1,0:T(8,128)(2,1)S(1)}, bf16[16,2048]{1,0:T(8,128)(2,1)S(1)}, u32[]{:S(2)}, u32[]{:S(2)}) collective-permute-start(bf16[16,2048]{1,0:T(8,128)(2,1)S(1)} %get-tuple-element.140), channel_id=1, source_target_pairs={{0,4},{1,5},{2,6},{3,7},{4,0},{5,1},{6,2},{7,3},{8,12},{9,13},{10,... | collective-permute-start | bytes 196616 | tf_op jit(solution)/shard_map/ppermute | solution.py:711
  31.8 5.2 %collective-permute-start.10 = (bf16[16,2048]{1,0:T(8,128)(2,1)S(1)}, bf16[16,2048]{1,0:T(8,128)(2,1)S(1)}, u32[]{:S(2)}, u32[]{:S(2)}) collective-permute-start(bf16[16,2048]{1,0:T(8,128)(2,1)S(1)} %get-tuple-element.141), channel_id=1, source_target_pairs={{0,2},{1,3},{2,0},{3,1},{4,6},{5,7},{6,4},{7,5},{8,10},{9,11},{10,... | collective-permute-start | bytes 196616 | tf_op jit(solution)/shard_map/ppermute | solution.py:711
  34.7 6.2 %collective-permute-start.11 = (bf16[16,2048]{1,0:T(8,128)(2,1)S(1)}, bf16[16,2048]{1,0:T(8,128)(2,1)S(1)}, u32[]{:S(2)}, u32[]{:S(2)}) collective-permute-start(bf16[16,2048]{1,0:T(8,128)(2,1)S(1)} %get-tuple-element.142), channel_id=1, source_target_pairs={{0,7},{1,6},{2,5},{3,4},{4,3},{5,2},{6,1},{7,0},{8,15},{9,14},{10,... | collective-permute-start | bytes 196616 | tf_op jit(solution)/shard_map/ppermute | solution.py:711
  36.9 6.6 %collective-permute-start.12 = (bf16[16,2048]{1,0:T(8,128)(2,1)S(1)}, bf16[16,2048]{1,0:T(8,128)(2,1)S(1)}, u32[]{:S(2)}, u32[]{:S(2)}) collective-permute-start(bf16[16,2048]{1,0:T(8,128)(2,1)S(1)} %get-tuple-element.143), channel_id=1, source_target_pairs={{0,5},{1,4},{2,7},{3,6},{4,1},{5,0},{6,3},{7,2},{8,13},{9,12},{10,... | collective-permute-start | bytes 196616 | tf_op jit(solution)/shard_map/ppermute | solution.py:711
  36.9 6.6 %collective-permute-start.13 = (bf16[16,2048]{1,0:T(8,128)(2,1)S(1)}, bf16[16,2048]{1,0:T(8,128)(2,1)S(1)}, u32[]{:S(2)}, u32[]{:S(2)}) collective-permute-start(bf16[16,2048]{1,0:T(8,128)(2,1)S(1)} %get-tuple-element.144), channel_id=1, source_target_pairs={{0,3},{1,2},{2,1},{3,0},{4,7},{5,6},{6,5},{7,4},{8,11},{9,10},{10,... | collective-permute-start | bytes 196616 | tf_op jit(solution)/shard_map/ppermute | solution.py:711
  40.9 2.6 %collective-permute-start.14 = (bf16[16,2048]{1,0:T(8,128)(2,1)S(1)}, bf16[16,2048]{1,0:T(8,128)(2,1)S(1)}, u32[]{:S(2)}, u32[]{:S(2)}) collective-permute-start(bf16[16,2048]{1,0:T(8,128)(2,1)S(1)} %get-tuple-element.145), channel_id=1, source_target_pairs={{0,1},{1,0},{2,3},{3,2},{4,5},{5,4},{6,7},{7,6},{8,9},{9,8},{10,11... | collective-permute-start | bytes 196616 | tf_op jit(solution)/shard_map/ppermute | solution.py:711
  43.6 5.2 %copy-start.2 = (bf16[1024,768]{1,0:T(8,128)(2,1)S(1)}, bf16[1024,768]{1,0:T(8,128)(2,1)}, u32[]{:S(2)}) copy-start(bf16[1024,768]{1,0:T(8,128)(2,1)} %refs_0_.5) | copy-start | bytes 4718596
  43.6 5.2 %copy-start.4 = (bf16[768,192]{0,1:T(8,128)(2,1)S(1)}, bf16[768,192]{0,1:T(8,128)(2,1)}, u32[]{:S(2)}) copy-start(bf16[768,192]{0,1:T(8,128)(2,1)} %param.18) | copy-start | bytes 884740
  43.6 5.2 %copy-start.5 = (bf16[768,192]{0,1:T(8,128)(2,1)S(1)}, bf16[768,192]{0,1:T(8,128)(2,1)}, u32[]{:S(2)}) copy-start(bf16[768,192]{0,1:T(8,128)(2,1)} %param.19) | copy-start | bytes 884740
  43.6 5.2 %copy-start.6 = (bf16[768,192]{0,1:T(8,128)(2,1)S(1)}, bf16[768,192]{0,1:T(8,128)(2,1)}, u32[]{:S(2)}) copy-start(bf16[768,192]{0,1:T(8,128)(2,1)} %param.20) | copy-start | bytes 884740
  45.2 9.1 %collective-permute-start.15 = (bf16[160,384]{1,0:T(8,128)(2,1)S(1)}, bf16[160,384]{1,0:T(8,128)(2,1)S(1)}, u32[]{:S(2)}, u32[]{:S(2)}) collective-permute-start(bf16[160,384]{1,0:T(8,128)(2,1)S(1)} %get-tuple-element.148), channel_id=1, source_target_pairs={{0,8},{8,0},{16,24},{24,16},{1,9},{9,1},{17,25},{25,17},{2,10},{10... | collective-permute-start | bytes 368648 | tf_op jit(solution)/shard_map/ppermute | solution.py:711
  46.8 7.7 %collective-permute-start.16 = (bf16[160,384]{1,0:T(8,128)(2,1)S(1)}, bf16[160,384]{1,0:T(8,128)(2,1)S(1)}, u32[]{:S(2)}, u32[]{:S(2)}) collective-permute-start(bf16[160,384]{1,0:T(8,128)(2,1)S(1)} %get-tuple-element.149), channel_id=1, source_target_pairs={{0,16},{8,24},{16,0},{24,8},{1,17},{9,25},{17,1},{25,9},{2,18},{10... | collective-permute-start | bytes 368648 | tf_op jit(solution)/shard_map/ppermute | solution.py:711
  47.3 7.2 %collective-permute-start.17 = (bf16[160,384]{1,0:T(8,128)(2,1)S(1)}, bf16[160,384]{1,0:T(8,128)(2,1)S(1)}, u32[]{:S(2)}, u32[]{:S(2)}) collective-permute-start(bf16[160,384]{1,0:T(8,128)(2,1)S(1)} %get-tuple-element.150), channel_id=1, source_target_pairs={{0,24},{8,16},{16,8},{24,0},{1,25},{9,17},{17,9},{25,1},{2,26},{10... | collective-permute-start | bytes 368648 | tf_op jit(solution)/shard_map/ppermute | solution.py:711
  54.6 12.6 %collective-permute-start.18 = (bf16[192,1024]{1,0:T(8,128)(2,1)S(1)}, bf16[192,1024]{1,0:T(8,128)(2,1)S(1)}, u32[]{:S(2)}, u32[]{:S(2)}) collective-permute-start(bf16[192,1024]{1,0:T(8,128)(2,1)S(1)} %get-tuple-element.163), channel_id=1, source_target_pairs={{0,24},{8,16},{16,8},{24,0},{1,25},{9,17},{17,9},{25,1},{2,26},{10... | collective-permute-start | bytes 1179656 | tf_op jit(solution)/shard_map/ppermute | solution.py:711
  56.0 5.7 %collective-permute-start.19 = (bf16[20,384]{1,0:T(8,128)(2,1)S(1)}, bf16[20,384]{1,0:T(8,128)(2,1)S(1)}, u32[]{:S(2)}, u32[]{:S(2)}) collective-permute-start(bf16[20,384]{1,0:T(8,128)(2,1)S(1)} %get-tuple-element.168), channel_id=1, source_target_pairs={{0,6},{1,7},{2,4},{3,5},{4,2},{5,3},{6,0},{7,1},{8,14},{9,15},{10,... | collective-permute-start | bytes 46088 | tf_op jit(solution)/shard_map/ppermute | solution.py:711
  57.8 4.7 %collective-permute-start.20 = (bf16[20,384]{1,0:T(8,128)(2,1)S(1)}, bf16[20,384]{1,0:T(8,128)(2,1)S(1)}, u32[]{:S(2)}, u32[]{:S(2)}) collective-permute-start(bf16[20,384]{1,0:T(8,128)(2,1)S(1)} %get-tuple-element.169), channel_id=1, source_target_pairs={{0,4},{1,5},{2,6},{3,7},{4,0},{5,1},{6,2},{7,3},{8,12},{9,13},{10,... | collective-permute-start | bytes 46088 | tf_op jit(solution)/shard_map/ppermute | solution.py:711
  58.3 5.6 %collective-permute-start.21 = (bf16[20,384]{1,0:T(8,128)(2,1)S(1)}, bf16[20,384]{1,0:T(8,128)(2,1)S(1)}, u32[]{:S(2)}, u32[]{:S(2)}) collective-permute-start(bf16[20,384]{1,0:T(8,128)(2,1)S(1)} %get-tuple-element.170), channel_id=1, source_target_pairs={{0,2},{1,3},{2,0},{3,1},{4,6},{5,7},{6,4},{7,5},{8,10},{9,11},{10,... | collective-permute-start | bytes 46088 | tf_op jit(solution)/shard_map/ppermute | solution.py:711
  60.4 6.8 %collective-permute-start.22 = (bf16[20,384]{1,0:T(8,128)(2,1)S(1)}, bf16[20,384]{1,0:T(8,128)(2,1)S(1)}, u32[]{:S(2)}, u32[]{:S(2)}) collective-permute-start(bf16[20,384]{1,0:T(8,128)(2,1)S(1)} %get-tuple-element.171), channel_id=1, source_target_pairs={{0,7},{1,6},{2,5},{3,4},{4,3},{5,2},{6,1},{7,0},{8,15},{9,14},{10,... | collective-permute-start | bytes 46088 | tf_op jit(solution)/shard_map/ppermute | solution.py:711
  61.6 5.5 %collective-permute-start.23 = (bf16[20,384]{1,0:T(8,128)(2,1)S(1)}, bf16[20,384]{1,0:T(8,128)(2,1)S(1)}, u32[]{:S(2)}, u32[]{:S(2)}) collective-permute-start(bf16[20,384]{1,0:T(8,128)(2,1)S(1)} %get-tuple-element.172), channel_id=1, source_target_pairs={{0,5},{1,4},{2,7},{3,6},{4,1},{5,0},{6,3},{7,2},{8,13},{9,12},{10,... | collective-permute-start | bytes 46088 | tf_op jit(solution)/shard_map/ppermute | solution.py:711
  62.5 4.7 %collective-permute-start.24 = (bf16[20,384]{1,0:T(8,128)(2,1)S(1)}, bf16[20,384]{1,0:T(8,128)(2,1)S(1)}, u32[]{:S(2)}, u32[]{:S(2)}) collective-permute-start(bf16[20,384]{1,0:T(8,128)(2,1)S(1)} %get-tuple-element.173), channel_id=1, source_target_pairs={{0,3},{1,2},{2,1},{3,0},{4,7},{5,6},{6,5},{7,4},{8,11},{9,10},{10,... | collective-permute-start | bytes 46088 | tf_op jit(solution)/shard_map/ppermute | solution.py:711
  63.9 3.3 %collective-permute-start.25 = (bf16[20,384]{1,0:T(8,128)(2,1)S(1)}, bf16[20,384]{1,0:T(8,128)(2,1)S(1)}, u32[]{:S(2)}, u32[]{:S(2)}) collective-permute-start(bf16[20,384]{1,0:T(8,128)(2,1)S(1)} %get-tuple-element.174), channel_id=1, source_target_pairs={{0,1},{1,0},{2,3},{3,2},{4,5},{5,4},{6,7},{7,6},{8,9},{9,8},{10,11... | collective-permute-start | bytes 46088 | tf_op jit(solution)/shard_map/ppermute | solution.py:711
  67.2 7.2 %collective-permute-start.28 = (bf16[160,384]{1,0:T(8,128)(2,1)S(1)}, bf16[160,384]{1,0:T(8,128)(2,1)S(1)}, u32[]{:S(2)}, u32[]{:S(2)}) collective-permute-start(bf16[160,384]{1,0:T(8,128)(2,1)S(1)} %get-tuple-element.178.refs_0_), channel_id=1, source_target_pairs={{0,24},{8,16},{16,8},{24,0},{1,25},{9,17},{17,9},{25,1},{2,26},{10... | collective-permute-start | bytes 368648 | tf_op jit(solution)/shard_map/ppermute | solution.py:711
  68.9 7.1 %collective-permute-start.27 = (bf16[160,384]{1,0:T(8,128)(2,1)S(1)}, bf16[160,384]{1,0:T(8,128)(2,1)S(1)}, u32[]{:S(2)}, u32[]{:S(2)}) collective-permute-start(bf16[160,384]{1,0:T(8,128)(2,1)S(1)} %get-tuple-element.178.refs_0_), channel_id=1, source_target_pairs={{0,16},{8,24},{16,0},{24,8},{1,17},{9,25},{17,1},{25,9},{2,18},{10... | collective-permute-start | bytes 368648 | tf_op jit(solution)/shard_map/ppermute | solution.py:711
  69.5 6.7 %collective-permute-start.26 = (bf16[160,384]{1,0:T(8,128)(2,1)S(1)}, bf16[160,384]{1,0:T(8,128)(2,1)S(1)}, u32[]{:S(2)}, u32[]{:S(2)}) collective-permute-start(bf16[160,384]{1,0:T(8,128)(2,1)S(1)} %get-tuple-element.178.refs_0_), channel_id=1, source_target_pairs={{0,8},{8,0},{16,24},{24,16},{1,9},{9,1},{17,25},{25,17},{2,10},{10... | collective-permute-start | bytes 368648 | tf_op jit(solution)/shard_map/ppermute | solution.py:711
  73.3 5.2 %copy-start.10 = (f32[768]{0:T(1024)S(1)}, f32[768]{0:T(1024)}, u32[]{:S(2)}) copy-start(f32[768]{0:T(1024)} %refs_11_.3) | copy-start | bytes 9220
  82.7 3.0 %copy-start.11 = (s32[2047]{0:T(1024)S(1)}, s32[2047]{0:T(1024)}, u32[]{:S(2)}) copy-start(s32[2047]{0:T(1024)} %param.29) | copy-start | bytes 24568
  82.7 2.3 %collective-permute-start.29 = (bf16[384,768]{1,0:T(8,128)(2,1)S(1)}, bf16[384,768]{1,0:T(8,128)(2,1)S(1)}, u32[]{:S(2)}, u32[]{:S(2)}) collective-permute-start(bf16[384,768]{1,0:T(8,128)(2,1)S(1)} %get-tuple-element.204), channel_id=1, source_target_pairs={{0,1},{1,0},{2,3},{3,2},{4,5},{5,4},{6,7},{7,6},{8,9},{9,8},{10,11... | collective-permute-start | bytes 1769480 | tf_op jit(solution)/shard_map/ppermute | solution.py:711
  82.7 12.1 %collective-permute-start.31 = (bf16[272,768]{1,0:T(8,128)(2,1)S(1)}, bf16[272,768]{1,0:T(8,128)(2,1)S(1)}, u32[]{:S(2)}, u32[]{:S(2)}) collective-permute-start(bf16[272,768]{1,0:T(8,128)(2,1)S(1)} %get-tuple-element.208), channel_id=1, source_target_pairs={{0,8},{8,0},{16,24},{24,16},{1,9},{9,1},{17,25},{25,17},{2,10},{10... | collective-permute-start | bytes 1253384 | tf_op jit(solution)/shard_map/ppermute | solution.py:711
  83.5 11.2 %collective-permute-start.32 = (bf16[256,768]{1,0:T(8,128)(2,1)S(1)}, bf16[256,768]{1,0:T(8,128)(2,1)S(1)}, u32[]{:S(2)}, u32[]{:S(2)}) collective-permute-start(bf16[256,768]{1,0:T(8,128)(2,1)S(1)} %get-tuple-element.210), channel_id=1, source_target_pairs={{0,16},{8,24},{16,0},{24,8},{1,17},{9,25},{17,1},{25,9},{2,18},{10... | collective-permute-start | bytes 1179656 | tf_op jit(solution)/shard_map/ppermute | solution.py:711
  85.1 9.7 %collective-permute-start.30 = (bf16[192,768]{1,0:T(8,128)(2,1)S(1)}, bf16[192,768]{1,0:T(8,128)(2,1)S(1)}, u32[]{:S(2)}, u32[]{:S(2)}) collective-permute-start(bf16[192,768]{1,0:T(8,128)(2,1)S(1)} %get-tuple-element.206), channel_id=1, source_target_pairs={{0,2},{1,3},{2,0},{3,1},{4,6},{5,7},{6,4},{7,5},{8,10},{9,11},{10,... | collective-permute-start | bytes 884744 | tf_op jit(solution)/shard_map/ppermute | solution.py:711
  95.1 11.0 %collective-permute-start.34 = (bf16[144,768]{1,0:T(8,128)(2,1)S(1)}, bf16[144,768]{1,0:T(8,128)(2,1)S(1)}, u32[]{:S(2)}, u32[]{:S(2)}) collective-permute-start(bf16[144,768]{1,0:T(8,128)(2,1)S(1)} %get-tuple-element.224.refs_5_), channel_id=1, source_target_pairs={{0,16},{8,24},{16,0},{24,8},{1,17},{9,25},{17,1},{25,9},{2,18},{10... | collective-permute-start | bytes 663560 | tf_op jit(solution)/shard_map/ppermute | solution.py:711
  96.5 9.6 %collective-permute-start.33 = (bf16[128,768]{1,0:T(8,128)(2,1)S(1)}, bf16[128,768]{1,0:T(8,128)(2,1)S(1)}, u32[]{:S(2)}, u32[]{:S(2)}) collective-permute-start(bf16[128,768]{1,0:T(8,128)(2,1)S(1)} %get-tuple-element.223), channel_id=1, source_target_pairs={{0,8},{8,0},{16,24},{24,16},{1,9},{9,1},{17,25},{25,17},{2,10},{10... | collective-permute-start | bytes 589832 | tf_op jit(solution)/shard_map/ppermute | solution.py:711
  97.3 8.8 %collective-permute-start.35 = (bf16[96,768]{1,0:T(8,128)(2,1)S(1)}, bf16[96,768]{1,0:T(8,128)(2,1)S(1)}, u32[]{:S(2)}, u32[]{:S(2)}) collective-permute-start(bf16[96,768]{1,0:T(8,128)(2,1)S(1)} %get-tuple-element.231), channel_id=1, source_target_pairs={{0,4},{1,5},{2,6},{3,7},{4,0},{5,1},{6,2},{7,3},{8,12},{9,13},{10,... | collective-permute-start | bytes 442376 | tf_op jit(solution)/shard_map/ppermute | solution.py:711
  106.8 11.4 %collective-permute-start.38 = (bf16[256,768]{1,0:T(8,128)(2,1)S(1)}, bf16[256,768]{1,0:T(8,128)(2,1)S(1)}, u32[]{:S(2)}, u32[]{:S(2)}) collective-permute-start(bf16[256,768]{1,0:T(8,128)(2,1)S(1)} %get-tuple-element.236.own), channel_id=1, source_target_pairs={{0,16},{8,24},{16,0},{24,8},{1,17},{9,25},{17,1},{25,9},{2,18},{10... | collective-permute-start | bytes 1179656 | tf_op jit(solution)/shard_map/ppermute | solution.py:711
  107.7 10.4 %collective-permute-start.37 = (bf16[256,768]{1,0:T(8,128)(2,1)S(1)}, bf16[256,768]{1,0:T(8,128)(2,1)S(1)}, u32[]{:S(2)}, u32[]{:S(2)}) collective-permute-start(bf16[256,768]{1,0:T(8,128)(2,1)S(1)} %get-tuple-element.236.own), channel_id=1, source_target_pairs={{0,8},{8,0},{16,24},{24,16},{1,9},{9,1},{17,25},{25,17},{2,10},{10... | collective-permute-start | bytes 1179656 | tf_op jit(solution)/shard_map/ppermute | solution.py:711
  108.9 9.3 %collective-permute-start.36 = (bf16[112,768]{1,0:T(8,128)(2,1)S(1)}, bf16[112,768]{1,0:T(8,128)(2,1)S(1)}, u32[]{:S(2)}, u32[]{:S(2)}) collective-permute-start(bf16[112,768]{1,0:T(8,128)(2,1)S(1)} %get-tuple-element.235.refs_0_), channel_id=1, source_target_pairs={{0,4},{1,5},{2,6},{3,7},{4,0},{5,1},{6,2},{7,3},{8,12},{9,13},{10,... | collective-permute-start | bytes 516104 | tf_op jit(solution)/shard_map/ppermute | solution.py:711
  118.8 9.5 %collective-permute-start.41 = (bf16[208,768]{1,0:T(8,128)(2,1)S(1)}, bf16[208,768]{1,0:T(8,128)(2,1)S(1)}, u32[]{:S(2)}, u32[]{:S(2)}) collective-permute-start(bf16[208,768]{1,0:T(8,128)(2,1)S(1)} %get-tuple-element.241.refs_0_), channel_id=1, source_target_pairs={{0,2},{1,3},{2,0},{3,1},{4,6},{5,7},{6,4},{7,5},{8,10},{9,11},{10,... | collective-permute-start | bytes 958472 | tf_op jit(solution)/shard_map/ppermute | solution.py:711
  118.8 6.8 %collective-permute-start.39 = (bf16[128,768]{1,0:T(8,128)(2,1)S(1)}, bf16[128,768]{1,0:T(8,128)(2,1)S(1)}, u32[]{:S(2)}, u32[]{:S(2)}) collective-permute-start(bf16[128,768]{1,0:T(8,128)(2,1)S(1)} %get-tuple-element.238), channel_id=1, source_target_pairs={{0,8},{8,0},{16,24},{24,16},{1,9},{9,1},{17,25},{25,17},{2,10},{10... | collective-permute-start | bytes 589832 | tf_op jit(solution)/shard_map/ppermute | solution.py:711
  120.1 5.8 %collective-permute-start.40 = (bf16[128,768]{1,0:T(8,128)(2,1)S(1)}, bf16[128,768]{1,0:T(8,128)(2,1)S(1)}, u32[]{:S(2)}, u32[]{:S(2)}) collective-permute-start(bf16[128,768]{1,0:T(8,128)(2,1)S(1)} %get-tuple-element.239), channel_id=1, source_target_pairs={{0,16},{8,24},{16,0},{24,8},{1,17},{9,25},{17,1},{25,9},{2,18},{10... | collective-permute-start | bytes 589832 | tf_op jit(solution)/shard_map/ppermute | solution.py:711
  128.9 2.0 %collective-permute-start.42 = (bf16[400,768]{1,0:T(8,128)(2,1)S(1)}, bf16[400,768]{1,0:T(8,128)(2,1)S(1)}, u32[]{:S(2)}, u32[]{:S(2)}) collective-permute-start(bf16[400,768]{1,0:T(8,128)(2,1)S(1)} %get-tuple-element.243.refs_0_), channel_id=1, source_target_pairs={{0,1},{1,0},{2,3},{3,2},{4,5},{5,4},{6,7},{7,6},{8,9},{9,8},{10,11... | collective-permute-start | bytes 1843208 | tf_op jit(solution)/shard_map/ppermute | solution.py:711
